TPU v7x, 32 devices: a whole 2x2x4 slice. The times are simulated.
32 devices in a mesh: grp: 1, pool: 1, ep: 8 (over z, y), tp: 4 (over x, core).
Axes of the slice: x: 2, y: 2, z: 4, core: 2. Of those that a mesh axis runs over, the one named last changes fastest.
Arguments:
- queries: bfloat16 [1024, 4096], P(('grp', 'ep'), ('pool', 'tp')), may hold values from -6 to 6
- keys_values: bfloat16 [1024, 1024], P(('grp', 'ep'), 'pool'), may hold values from -6 to 6
- residual: bfloat16 [1024, 2048], P(('grp', 'ep', 'tp'), 'pool'), may hold values from -24 to 24
- norm_gain: float32 [2048], P('pool'), may hold values from 0.1 to 1.9
- w_out: bfloat16 [4096, 2048], P(('pool', 'tp')), may hold values from -0.75 to 0.75
- w_gate_up: bfloat16 [32, 2048, 768], P(('ep', 'tp'), 'pool'), may hold values from -0.125 to 0.125
- w_down: bfloat16 [32, 384, 2048], P(('ep', 'tp'), None, 'pool'), may hold values from -0.3125 to 0.3125
- expert_ids: int32 [1024, 8], P(('grp', 'ep', 'tp')), may hold values from 0 to 31, as said below
- mix_weights: float32 [1024, 8], P(('grp', 'ep', 'tp')), may hold values from 0.1 to 1
- clip_lengths: int32 [3], P('grp'), may hold values from 129 to 512, as said below
Outputs:
- layer_out: bfloat16 [1024, 2048], P(('grp', 'ep', 'tp'), 'pool')
Inputs may be any that keep to these rules, and one draw needn't show every extreme that they name: `clip_lengths`: 3 clips cover the 1024 tokens; one clip has exactly 512 tokens. `expert_ids`: each row names 8 different experts. Among the 32 rows of one device (aligned blocks of rows) no expert is named more than 16 times, and one expert is named exactly 16 times in every block.
All inputs are finite; a program needn't handle non-finite values.
Results may differ from a plain program's by a relative error of at most 0.018.
Values may be sent and summed in bfloat16 or wider, within the bound.
A program may use at most 64 MiB of HBM per device.

v0:
```python
import jax
import jax.numpy as jnp
from jax import lax
from jax.sharding import PartitionSpec as P

D = 2048
QH = 32
KVH = 4
HD = 128


def clip_index(clip_lengths, places):
    ends = jnp.cumsum(clip_lengths)
    return jnp.sum((places[:, None] >= ends[None, :]).astype(jnp.int32), axis=1)


def body(
    queries,
    keys_values,
    residual,
    norm_gain,
    w_out,
    w_gate_up,
    w_down,
    expert_ids,
    mix_weights,
    clip_lengths,
):
    rows = queries.shape[0]
    heads_here = queries.shape[1] // HD
    pool_size = lax.axis_size("pool")
    tensor_size = lax.axis_size("tp")
    context_size = lax.axis_size("ep")
    pool_index = lax.axis_index("pool")
    tensor_index = lax.axis_index("tp")
    pair_heads = keys_values.shape[1] // (2 * HD)
    group = QH // KVH
    head_pick = (
        pool_index * tensor_size + tensor_index
    ) * heads_here // group - pool_index * pair_heads
    own_pairs = lax.dynamic_slice_in_dim(keys_values, head_pick * (2 * HD), 2 * HD, 1)
    places = lax.axis_index("ep") * rows + jnp.arange(rows, dtype=jnp.int32)
    query_clip = clip_index(clip_lengths, places)
    query_heads = queries.reshape(rows, heads_here, HD)
    scale = HD ** (-0.5)
    start_state = (
        jnp.full((heads_here, rows), -1e30, jnp.float32),
        jnp.zeros((heads_here, rows), jnp.float32),
        jnp.zeros((heads_here, rows, HD), jnp.float32),
    )
    piece = lax.all_gather(own_pairs, "ep", axis=0, tiled=True)
    length = piece.shape[0]
    stride = min(length, rows * max(1, 512 // rows))
    while length % stride:
        stride = stride - 1

    def one_block(index, state):
        top, total, numer = state
        block = lax.dynamic_slice_in_dim(piece, index * stride, stride, 0)
        key_clip = clip_index(clip_lengths, index * stride + jnp.arange(stride, dtype=jnp.int32))
        scores = (
            jnp.einsum(
                "rhd,nd->hrn", query_heads, block[:, :HD], preferred_element_type=jnp.float32
            )
            * scale
        )
        same = (query_clip[:, None] == key_clip[None, :])[None, :, :]
        new_top = jnp.maximum(top, jnp.max(jnp.where(same, scores, -1e30), axis=2))
        weights = jnp.where(same, jnp.exp(scores - new_top[:, :, None]), 0.0)
        factor = jnp.exp(top - new_top)
        total = total * factor + jnp.sum(weights, axis=2)
        numer = numer * factor[:, :, None] + jnp.einsum(
            "hrn,nd->hrd",
            weights.astype(jnp.bfloat16),
            block[:, HD:],
            preferred_element_type=jnp.float32,
        )
        return (new_top, total, numer)

    top, total, numer = lax.fori_loop(0, length // stride, one_block, start_state)
    attended = (numer / total[:, :, None]).astype(jnp.bfloat16)
    half = residual.shape[1]
    out_heads = w_out.reshape(heads_here, HD, pool_size * half)
    moe_rows = residual.shape[0]
    start = jnp.int32(0)
    pieces = []
    for offset in range(lax.axis_size(("pool", "tp")) * moe_rows // rows):
        part = start // rows + offset
        weights = lax.dynamic_slice_in_dim(out_heads, part * half, half, 2)
        pieces.append(
            jnp.einsum("hrd,hde->re", attended, weights, preferred_element_type=jnp.float32)
        )
    mixed = lax.psum_scatter(
        jnp.concatenate(pieces, axis=0).astype(jnp.bfloat16),
        ("pool", "tp"),
        scatter_dimension=0,
        tiled=True,
    ).astype(jnp.float32)
    hidden_state = residual.astype(jnp.float32) + mixed
    squares = lax.psum(jnp.sum(hidden_state * hidden_state, axis=1), "pool")
    normed = (hidden_state * lax.rsqrt(squares / D + 1e-06)[:, None] * norm_gain[None, :]).astype(
        jnp.bfloat16
    )
    top_k = expert_ids.shape[1]
    local_experts = w_gate_up.shape[0]
    experts = local_experts * context_size * tensor_size
    capacity = 2 * moe_rows * top_k // experts
    flat = expert_ids.reshape(-1)
    marks = (flat[:, None] == jnp.arange(experts, dtype=jnp.int32)[None, :]).astype(jnp.int32)
    rank = jnp.sum(jnp.cumsum(marks, axis=0) * marks, axis=1) - 1
    slot = flat * capacity + rank
    source = jnp.arange(moe_rows * top_k, dtype=jnp.int32) // top_k
    outgoing = jnp.zeros((experts * capacity, half), jnp.bfloat16).at[slot].set(normed[source])
    hidden_width = w_down.shape[1]
    shaped = outgoing.reshape(experts, capacity, half)
    arrived = lax.all_to_all(shaped, ("ep", "tp"), split_axis=0, concat_axis=0, tiled=True)
    width = arrived.shape[1]
    grouped = arrived.reshape(-1, local_experts, width, half)
    both = jnp.einsum("slcd,ldf->slcf", grouped, w_gate_up, preferred_element_type=jnp.float32)
    both = lax.psum(both.astype(jnp.bfloat16), "pool").astype(jnp.float32)
    hidden = (jax.nn.silu(both[..., :hidden_width]) * both[..., hidden_width:]).astype(jnp.bfloat16)
    result = jnp.einsum(
        "slcf,lfd->slcd", hidden, w_down, preferred_element_type=jnp.float32
    ).astype(jnp.bfloat16)
    finished = result.reshape(-1, width, half)
    back = lax.all_to_all(finished, ("ep", "tp"), split_axis=0, concat_axis=0, tiled=True)
    back_rows = back.reshape(experts * capacity, half)[slot]
    gathered = back_rows.reshape(moe_rows, top_k, half).astype(jnp.float32)
    blended = jnp.sum(gathered * mix_weights[:, :, None], axis=1)
    return (hidden_state + blended).astype(jnp.bfloat16)


def solution(mesh):
    placed = (
        P(("grp", "ep"), ("pool", "tp")),
        P(("grp", "ep"), "pool"),
        P(("grp", "ep", "tp"), "pool"),
        P("pool"),
        P(("pool", "tp"), None),
        P(("ep", "tp"), "pool", None),
        P(("ep", "tp"), None, "pool"),
        P(("grp", "ep", "tp"), None),
        P(("grp", "ep", "tp"), None),
        P("grp"),
    )
    return jax.shard_map(
        body, mesh=mesh, in_specs=placed, out_specs=P(("grp", "ep", "tp"), "pool"), check_vma=False
    )
```

profile of v0, /device:TPU:0, one launch (start us, length us, event | category | flops | bytes accessed | tf_op | source)
XLA Modules:
  0.0 224.2 jit_solution(7995391361018483164)
XLA Ops:
  6.5 1.0 constant_dynamic-slice_fusion
  7.5 35.2 %all_gather.3 = bf16[1024,256]{1,0:T(8,128)(2,1)} all-gather(bf16[128,256]{1,0:T(8,128)(2,1)S(1)} %constant_dynamic-slice_fusion), channel_id=1, replica_groups=mesh['grp'=1,'pool'=1,'ep'=8,'tp'=4] {'ep'}, dimensions={0}, use_global_device_ids=true | all-gather | bytes 589824 | tf_op jit(solution)/shard_map/all_gather | solution.py:51
  42.8 0.8 broadcast_in_dim.93
  43.6 1.8 copy.22
  45.4 1.1 copy.23
  46.6 16.3 %while.20 = (s32[]{:T(128)}, f32[8,128]{1,0:T(8,128)S(1)}, f32[8,128]{1,0:T(8,128)S(1)}, f32[8,128,128]{2,1,0:T(8,128)}, s32[128]{0:T(128)S(1)}, /*index=5*/s32[...) while((s32[]{:T(128)}, f32[8,128]{1,0:T(8,128)S(1)}, ...), condition=%wide.region_6.7_spmd.clone, body=%wide.region_2.6_spmd.clone.sunk | while | flops 274671104 | bytes 8200927 | solution.py:80
  46.7 0.1 broadcast_compare_fusion.2
  46.8 2.7 %fusion.50 = (f32[8,128]{1,0:T(8,128)S(1)}, f32[512,128,8]{1,0,2:T(8,128)}) fusion(pred[128,512]{0,1:T(8,128)(4,1)S(1)} %broadcast_compare_fusion.2, bf16[128,8,128]{2,0,1:T(8,128)(2,1)S(1)} %get-tuple-element.352, bf16[1024,256]{1,0:T(8,128)(2,1)} %get-tuple-element.351, s32[]{:T(128)S(6)} %select_n.100), kind=kOutput, calls=%fused_computation.5.clone.1 | convolution fusion | flops 135789568 | bytes 2560004 | tf_op jit(solution)/shard_map/while/body/eval_jaxpr/rhd,nd->hrn/dot_general | solution.py:62
  49.5 2.0 fusion.51
  51.6 3.1 %convolution_add_fusion.2 = f32[8,128,128]{2,1,0:T(8,128)} fusion(f32[512,128,8]{1,0,2:T(8,128)} %get-tuple-element.316, f32[8,128]{1,0:T(8,128)S(1)} %select_maximum_fusion.2, pred[128,512]{0,1:T(8,128)(4,1)S(1)} %broadcast_compare_fusion.2, f32[8,128,128]{2,1,0:T(8,128)} %get-tuple-element.335, f32[8,128]{1,0:T(8,128)S(1)} %get-tuple-element.318, ...), kind=kOutput, calls=%fused_computation.10.clone.1 | convolution fusion | flops 136708096 | bytes 3350537 | tf_op jit(solution)/shard_map/while/body/eval_jaxpr/hrn,nd->hrd/dot_general | solution.py:72
  54.8 0.1 broadcast_compare_fusion.2
  54.9 2.7 %fusion.50 = (f32[8,128]{1,0:T(8,128)S(1)}, f32[512,128,8]{1,0,2:T(8,128)}) fusion(pred[128,512]{0,1:T(8,128)(4,1)S(1)} %broadcast_compare_fusion.2, bf16[128,8,128]{2,0,1:T(8,128)(2,1)S(1)} %get-tuple-element.352, bf16[1024,256]{1,0:T(8,128)(2,1)} %get-tuple-element.351, s32[]{:T(128)S(6)} %select_n.100), kind=kOutput, calls=%fused_computation.5.clone.1 | convolution fusion | flops 135789568 | bytes 2560004 | tf_op jit(solution)/shard_map/while/body/eval_jaxpr/rhd,nd->hrn/dot_general | solution.py:62
  57.6 2.0 fusion.51
  59.7 3.2 %convolution_add_fusion.2 = f32[8,128,128]{2,1,0:T(8,128)} fusion(f32[512,128,8]{1,0,2:T(8,128)} %get-tuple-element.316, f32[8,128]{1,0:T(8,128)S(1)} %select_maximum_fusion.2, pred[128,512]{0,1:T(8,128)(4,1)S(1)} %broadcast_compare_fusion.2, f32[8,128,128]{2,1,0:T(8,128)} %get-tuple-element.335, f32[8,128]{1,0:T(8,128)S(1)} %get-tuple-element.318, ...), kind=kOutput, calls=%fused_computation.10.clone.1 | convolution fusion | flops 136708096 | bytes 3350537 | tf_op jit(solution)/shard_map/while/body/eval_jaxpr/hrn,nd->hrd/dot_general | solution.py:72
  62.9 3.9 %fusion.17 = bf16[128,2048]{1,0:T(8,128)(2,1)} fusion(bf16[8,128,2048]{2,1,0:T(8,128)(2,1)} %bitcast.105, f32[8,128,128]{2,1,0:T(8,128)} %get-tuple-element.197, f32[8,128]{1,0:T(8,128)S(1)} %get-tuple-element.198), kind=kOutput, calls=%fused_computation.33 | convolution fusion | flops 537395200 | bytes 5246976 | tf_op jit(solution)/shard_map/hrd,hde->re/dot_general | solution.py:91
  67.0 0.6 reduce-window.12
  67.6 0.2 slice_reduce_fusion
  67.8 0.1 eq.60
  68.0 0.1 mul.125
  68.2 0.1 fusion.37
  68.3 21.4 %reduce-scatter.2.cloned.1.call-done = bf16[32,2048]{1,0:T(8,128)(2,1)} async-done(((bf16[128,2048]{1,0:T(8,128)(2,1)}), bf16[32,2048]{1,0:T(8,128)(2,1)}) %reduce-scatter.2.cloned.1.call-update) | async-done | bytes 131088 | tf_op jit(solution)/shard_map/reduce_scatter | solution.py:93
  89.7 1.1 multiply_reduce_fusion
  90.7 1.0 multiply_convert_fusion
  91.7 7.1 %scatter_custom_fusion = bf16[512,2048]{1,0:T(8,128)(2,1)} fusion(s32[256]{0:T(256)S(1)} %bitcast.101, bf16[32,2048]{1,0:T(8,128)(2,1)S(1)} %multiply_convert_fusion, s32[1024]{0:T(1024)S(1)} %pad_clamp_fusion.1, bf16[]{:T(256)} %constant.154.clone.1), kind=kCustom, calls=%fused_computation.40 | custom fusion | bytes 2097154 | tf_op jit(solution)/shard_map/scatter | solution.py:113
  98.8 53.3 %all_to_all.10 = bf16[32,16,2048]{2,1,0:T(8,128)(2,1)S(1)} all-to-all(bf16[32,16,2048]{2,1,0:T(8,128)(2,1)} %bitcast.97), channel_id=1, replica_groups=mesh['grp'=1,'pool'=1,'ep'=8,'tp'=4] {'ep','tp'}, dimensions={0} | all-to-all | bytes 4194304 | tf_op jit(solution)/shard_map/all_to_all | solution.py:116
  152.1 1.8 fusion.26
  153.9 2.6 %convolution_convert_fusion = bf16[32,16,2048]{2,1,0:T(8,128)(2,1)} fusion(bf16[1,384,2048]{2,1,0:T(8,128)(2,1)S(1)} %copy-done.6, f32[32,1,16,768]{3,2,0,1:T(8,128)S(1)} %fusion.26), kind=kOutput, calls=%fused_computation.31 | convolution fusion | flops 807534592 | bytes 5242880 | tf_op jit(solution)/shard_map/slcf,lfd->slcd/dot_general | solution.py:122
  156.5 3.8 %all-to-all-start.1 = ((bf16[32,16,2048]{2,1,0:T(8,128)(2,1)}), bf16[32,16,2048]{2,1,0:T(8,128)(2,1)}, u32[]{:S(2)}, u32[]{:S(2)}) async-start(bf16[32,16,2048]{2,1,0:T(8,128)(2,1)} %convolution_convert_fusion), calls=%async_computation.2 | async-start | bytes 4194304 | tf_op jit(solution)/shard_map/all_to_all | solution.py:126
  160.4 48.8 %all-to-all-done.1 = bf16[32,16,2048]{2,1,0:T(8,128)(2,1)} async-done(((bf16[32,16,2048]{2,1,0:T(8,128)(2,1)}), bf16[32,16,2048]{2,1,0:T(8,128)(2,1)}, u32[]{:S(2)}, u32[]{:S(2)}) %all-to-all-start.1) | async-done | bytes 2097184 | tf_op jit(solution)/shard_map/all_to_all | solution.py:126
  209.2 5.2 %gather_fusion = bf16[256,2048]{1,0:T(8,128)(2,1)} fusion(bf16[512,2048]{1,0:T(8,128)(2,1)} %bitcast.20, s32[1024]{0:T(1024)S(1)} %pad_clamp_fusion), kind=kCustom, calls=%fused_computation.1 | custom fusion | bytes 2098176 | tf_op jit(solution)/shard_map/gather | solution.py:127
  214.4 2.2 fusion.18
  216.6 0.7 add_convert_fusion
  (45 shorter events, 0.8 us)
Async XLA Ops:
  6.5 145.6 %copy-start = (bf16[1,2048,768]{2,1,0:T(8,128)(2,1)S(1)}, bf16[1,2048,768]{2,1,0:T(8,128)(2,1)}, u32[]{:S(2)}) copy-start(bf16[1,2048,768]{2,1,0:T(8,128)(2,1)} %param.17) | copy-start | bytes 9437188
  6.5 83.1 %reduce-scatter.2.cloned.1.call-start = ((), (), s32[]{:S(2)}) async-start(), calls=%async_computation.3 | async-start | bytes 655360 | tf_op jit(solution)/shard_map/reduce_scatter | solution.py:93
  62.9 4.0 %copy-start.3 = (s32[32,8]{0,1:T(8,128)S(1)}, s32[32,8]{0,1:T(8,128)}, u32[]{:S(2)}) copy-start(s32[32,8]{0,1:T(8,128)} %param.19) | copy-start | bytes 3076
  62.9 26.8 %copy-start.1 = (bf16[32,2048]{1,0:T(8,128)(2,1)S(1)}, bf16[32,2048]{1,0:T(8,128)(2,1)}, u32[]{:S(2)}) copy-start(bf16[32,2048]{1,0:T(8,128)(2,1)} %param.14) | copy-start | bytes 393220
  62.9 27.9 %copy-start.4 = (f32[2048]{0:T(1024)S(1)}, f32[2048]{0:T(1024)}, u32[]{:S(2)}) copy-start(f32[2048]{0:T(1024)} %param.15) | copy-start | bytes 24580
  152.1 1.8 copy-start.6
  156.5 3.8 %copy-start.5 = (f32[32,8]{0,1:T(8,128)S(1)}, f32[32,8]{0,1:T(8,128)}, u32[]{:S(2)}) copy-start(f32[32,8]{0,1:T(8,128)} %param.20) | copy-start | bytes 3076
  156.5 52.7 %all-to-all-start.1 = ((bf16[32,16,2048]{2,1,0:T(8,128)(2,1)}), bf16[32,16,2048]{2,1,0:T(8,128)(2,1)}, u32[]{:S(2)}, u32[]{:S(2)}) async-start(bf16[32,16,2048]{2,1,0:T(8,128)(2,1)} %convolution_convert_fusion), calls=%async_computation.2 | async-start | bytes 4194304 | tf_op jit(solution)/shard_map/all_to_all | solution.py:126
  209.2 7.5 %copy-start.2 = (bf16[32,2048]{1,0:T(8,128)(2,1)S(1)}, bf16[32,2048]{1,0:T(8,128)(2,1)}, u32[]{:S(2)}) copy-start(bf16[32,2048]{1,0:T(8,128)(2,1)} %reduce-scatter.2.cloned.1.call-done) | copy-start | bytes 393220
Sparse Core Ops, SparseCore 0:
  67.0 22.6 reduce-scatter.1
where the time goes:
time: 225 us; the launch traced here: 224 us
  blocking collectives  88.5 us (39%)
  waiting for transfers between devices  70.2 us (31%)
  matrix products  20 us (9%)
  local copies, waits for them, and re-layouts  16.9 us (8%)
  between operations  13.5 us (6%)
  other arithmetic  11.2 us (5%)
  starting transfers between devices  3.79 us (2%)
    all_to_all x1, blocking collectives, body(): lax.all_to_all(shaped, ('ep', 'tp'), split_axis=0, concat_axis=0, tiled=T...  53.3 us
    all_to_all x1, waiting for transfers between devices, body(): lax.all_to_all(finished, ('ep', 'tp'), split_axis=0, concat_axis=0, tiled...  48.8 us
    all_gather x1, blocking collectives, body(): piece = lax.all_gather(own_pairs, 'ep', axis=0, tiled=True)  35.2 us
    reduce_scatter x1, waiting for transfers between devices, body(): lax.psum_scatter(jnp.concatenate(pieces, axis=0).astype(jnp.bfloat16), ('...  21.4 us
    scatter x1, local copies, waits for them, and re-layouts, body(): jnp.zeros((experts * capacity, half), jnp.bfloat16).at[slot]  7.06 us
    dot_general x2, matrix products, one_block(): jnp.einsum('hrn,nd->hrd', weights.astype(jnp.bfloat16), block[:, HD:], pr...  6.3 us
    dot_general x2, matrix products, one_block(): jnp.einsum('rhd,nd->hrn', query_heads, block[:, :HD], preferred_element_t...  5.41 us
    gather x1, local copies, waits for them, and re-layouts, body(): back_rows = back.reshape(experts * capacity, half)[slot]  5.24 us
  transfers between devices with their start and end apart: 2, of which 2 were waited for; matrix products, arithmetic and copies ran while one was open for 1% of the time, Pallas kernels for 0%

commit v1 on v0

--- a/solution.py
+++ b/solution.py
@@ -1,6 +1,10 @@
+import functools
+
 import jax
 import jax.numpy as jnp
 from jax import lax
+from jax.experimental import pallas as pl
+from jax.experimental.pallas import tpu as pltpu
 from jax.sharding import PartitionSpec as P
 
 D = 2048
@@ -12,6 +16,370 @@
 def clip_index(clip_lengths, places):
     ends = jnp.cumsum(clip_lengths)
     return jnp.sum((places[:, None] >= ends[None, :]).astype(jnp.int32), axis=1)
+
+
+def moe_kernel(
+    n_z,
+    n_experts,
+    parts,
+    send_ref,
+    hidden_ref,
+    wgu_hbm,
+    wd_hbm,
+    out_ref,
+    held,
+    wgu,
+    wd,
+    term,
+    pair_in,
+    relay_x,
+    relay_y,
+    from_x,
+    from_y,
+    from_z,
+    w_sem,
+    z_send,
+    z_recv,
+    x_send,
+    x_recv,
+    y_send,
+    y_recv,
+    da_send,
+    da_recv,
+    db_send,
+    db_recv,
+    sib_send,
+    sib_recv,
+    r_send,
+    r_recv,
+    rz_send,
+    rz_recv,
+):
+    ep = lax.axis_index("ep")
+    tp = lax.axis_index("tp")
+    z, y = ep // 2, ep % 2
+    x, c = tp // 2, tp % 2
+    rows = send_ref.shape[0]
+    half = hidden_ref.shape[1]
+    cut = half // 2
+    width = send_ref.shape[1]
+    first, second, rest = pl.ds(0, cut), pl.ds(cut, cut), pl.ds(cut, width - cut)
+    x_peer = (ep, (1 - x) * 2 + c)
+    y_peer = (z * 2 + 1 - y, tp)
+    sib = (ep, x * 2 + 1 - c)
+    q_own, q_x = x * 2 + y, (1 - x) * 2 + y
+    q_y, q_d = x * 2 + 1 - y, (1 - x) * 2 + 1 - y
+
+    load_gu = pltpu.make_async_copy(wgu_hbm.at[0], wgu, w_sem.at[0])
+    load_d = pltpu.make_async_copy(wd_hbm.at[0], wd, w_sem.at[1])
+    load_gu.start()
+    load_d.start()
+
+    barrier = pltpu.get_barrier_semaphore()
+    for peer in (x_peer, y_peer, sib):
+        pl.semaphore_signal(
+            barrier,
+            inc=1,
+            device_id={"ep": peer[0], "tp": peer[1]},
+            device_id_type=pl.DeviceIdType.MESH,
+        )
+    for step in range(1, n_z):
+        pl.semaphore_signal(
+            barrier,
+            inc=1,
+            device_id={"ep": ((z + step) % n_z) * 2 + y, "tp": tp},
+            device_id_type=pl.DeviceIdType.MESH,
+        )
+
+    def remote(src, dst, send, recv, peer):
+        return pltpu.make_async_remote_copy(
+            src_ref=src,
+            dst_ref=dst,
+            send_sem=send,
+            recv_sem=recv,
+            device_id={"ep": peer[0], "tp": peer[1]},
+            device_id_type=pl.DeviceIdType.MESH,
+        )
+
+    def along_z(block, up):
+        there = z + 1 if up else z - 1
+        return remote(
+            held.at[q_own, c, block],
+            held.at[q_own, c, block],
+            z_send.at[1 if up else 0, block],
+            z_recv.at[block],
+            (there * 2 + y, tp),
+        )
+
+    def over_x(q, block):
+        here = held.at[q, c, block]
+        return remote(here, here, x_send.at[block], x_recv.at[block], x_peer)
+
+    def over_y(q, block):
+        here = held.at[q, c, block]
+        return remote(here, here, y_send.at[block], y_recv.at[block], y_peer)
+
+    def diag_x(q, block):
+        here = held.at[q, c, block, :, first]
+        return remote(here, here, da_send.at[block], da_recv.at[block], x_peer)
+
+    def diag_y(q, block):
+        here = held.at[q, c, block, :, rest]
+        return remote(here, here, db_send.at[block], db_recv.at[block], y_peer)
+
+    def share(q, core, slot):
+        here = held.at[q, core]
+        return remote(here, here, sib_send.at[slot], sib_recv.at[slot], sib)
+
+    held[q_own, c, z] = send_ref[...]
+    pl.semaphore_wait(barrier, 3 + n_z - 1)
+
+    def each_at(distance, act):
+        if distance == 0:
+            act(z, 0)
+            return
+        pl.when(z - distance >= 0)(lambda: act(z - distance, -1))
+        pl.when(z + distance < n_z)(lambda: act(z + distance, 1))
+
+    def arrive_z(block, side):
+        if side:
+            along_z(block, side < 0).wait_recv()
+        if side <= 0:
+            pl.when(z + 1 < n_z)(lambda: along_z(block, True).start())
+        if side >= 0:
+            pl.when(z >= 1)(lambda: along_z(block, False).start())
+        over_x(q_own, block).start()
+        over_y(q_own, block).start()
+
+    def arrive_xy(block, side):
+        over_x(q_x, block).wait_recv()
+        diag_y(q_x, block).start()
+        over_y(q_y, block).wait_recv()
+        diag_x(q_y, block).start()
+
+    for distance in range(n_z + 1):
+        if distance < n_z:
+            each_at(distance, arrive_z)
+        if distance == n_z - 1:
+            share(q_own, c, 0).start()
+        if distance >= 1:
+            each_at(distance - 1, arrive_xy)
+    share(q_x, c, 1).start()
+    share(q_y, c, 2).start()
+    load_gu.wait()
+    load_d.wait()
+
+    mine = ep * lax.axis_size("tp") + tp
+    many = 2 * n_z * rows
+
+    def compute(q):
+        both = jnp.dot(
+            held[q, :, :, :, 0:half].reshape(many, half),
+            wgu[...],
+            preferred_element_type=jnp.float32,
+        )
+        ff = both.shape[1] // 2
+        gate, up = both[:, :ff], both[:, ff:]
+        acted = (gate / (1.0 + jnp.exp(-gate)) * up).astype(jnp.bfloat16)
+        shares = held[q, :, :, :, half:width].reshape(many, width - half).astype(jnp.float32)
+        lane = lax.broadcasted_iota(jnp.int32, shares.shape, 1)
+        wanted = lane == mine
+        for part in range(1, parts):
+            wanted = wanted | (lane == mine + part * n_experts)
+        mix = jnp.sum(jnp.where(wanted, shares, 0.0), axis=1, keepdims=True)
+        tile = half // 4
+        for at in range(0, half, tile):
+            result = jnp.dot(
+                acted, wd[:, at : at + tile], preferred_element_type=jnp.float32
+            ).astype(jnp.bfloat16)
+            term[q, :, :, at : at + tile] = (
+                (result.astype(jnp.float32) * mix)
+                .astype(jnp.bfloat16)
+                .reshape(2, n_z * rows, tile)
+            )
+
+    def pair(q, slot):
+        return remote(
+            term.at[q, 1 - c], pair_in.at[slot], sib_send.at[4 + slot], sib_recv.at[4 + slot], sib
+        )
+
+    def add_pair(q, slot):
+        pair(q, slot).wait_recv()
+        for at in range(0, half, cut):
+            to = pl.ds(at, cut)
+            term[q, c, :, to] = (
+                term[q, c, :, to].astype(jnp.float32) + pair_in[slot, :, to].astype(jnp.float32)
+            ).astype(jnp.bfloat16)
+
+    def reduce_x(q, columns, into, slot):
+        return remote(term.at[q, c, :, columns], into, r_send.at[slot], r_recv.at[slot], x_peer)
+
+    def reduce_y(q, columns, into, slot):
+        return remote(term.at[q, c, :, columns], into, r_send.at[slot], r_recv.at[slot], y_peer)
+
+    own_x = reduce_x(q_x, first, from_x.at[0], 0)
+    own_y = reduce_y(q_y, second, from_y.at[1], 1)
+    pass_x = reduce_x(q_d, first, relay_x, 2)
+    pass_y = reduce_y(q_d, second, relay_y, 3)
+    last_x = reduce_x(q_x, second, from_x.at[1], 4)
+    last_y = reduce_y(q_y, first, from_y.at[0], 5)
+
+    share(q_own, 1 - c, 0).wait_recv()
+    compute(q_own)
+    pair(q_own, 0).start()
+    share(q_x, 1 - c, 1).wait_recv()
+    compute(q_x)
+    pair(q_x, 1).start()
+    for block in range(n_z):
+        diag_x(q_d, block).wait_recv()
+        diag_y(q_d, block).wait_recv()
+    share(q_d, c, 3).start()
+    share(q_y, 1 - c, 2).wait_recv()
+    compute(q_y)
+    pair(q_y, 2).start()
+    add_pair(q_x, 1)
+    own_x.start()
+    share(q_d, 1 - c, 3).wait_recv()
+    compute(q_d)
+    pair(q_d, 3).start()
+    add_pair(q_y, 2)
+    own_y.start()
+    add_pair(q_d, 3)
+    pass_x.start()
+    pass_y.start()
+    add_pair(q_own, 0)
+
+    pass_x.wait_recv()
+    term[q_y, c, :, first] = (
+        term[q_y, c, :, first].astype(jnp.float32) + relay_x[...].astype(jnp.float32)
+    ).astype(jnp.bfloat16)
+    last_y.start()
+    pass_y.wait_recv()
+    term[q_x, c, :, second] = (
+        term[q_x, c, :, second].astype(jnp.float32) + relay_y[...].astype(jnp.float32)
+    ).astype(jnp.bfloat16)
+    last_x.start()
+
+    def finish(number, columns):
+        term[q_own, c, :, columns] = (
+            term[q_own, c, :, columns].astype(jnp.float32)
+            + from_x[number].astype(jnp.float32)
+            + from_y[number].astype(jnp.float32)
+        ).astype(jnp.bfloat16)
+
+    def deliver(number, columns, step):
+        there = (z + step) % n_z
+        return remote(
+            term.at[q_own, c, pl.ds(pl.multiple_of(there * rows, rows), rows), columns],
+            from_z.at[number, n_z - 1 - step],
+            rz_send.at[number, step - 1],
+            rz_recv.at[number, n_z - 1 - step],
+            (there * 2 + y, tp),
+        )
+
+    def collect(number, columns):
+        total = hidden_ref[:, columns] + term[
+            q_own, c, pl.ds(pl.multiple_of(z * rows, rows), rows), columns
+        ].astype(jnp.float32)
+        for slot in range(n_z - 1):
+            remote(
+                from_z.at[number, slot],
+                from_z.at[number, slot],
+                rz_send.at[number, slot],
+                rz_recv.at[number, slot],
+                sib,
+            ).wait_recv()
+            total = total + from_z[number, slot].astype(jnp.float32)
+        out_ref[:, columns] = total.astype(jnp.bfloat16)
+
+    own_x.wait_recv()
+    last_y.wait_recv()
+    finish(0, first)
+    for step in range(1, n_z):
+        deliver(0, first, step).start()
+    own_y.wait_recv()
+    last_x.wait_recv()
+    finish(1, second)
+    for step in range(1, n_z):
+        deliver(1, second, step).start()
+    collect(0, first)
+    collect(1, second)
+
+    for copy in (own_x, own_y, pass_x, pass_y, last_x, last_y):
+        copy.wait_send()
+    for slot, q in enumerate((q_own, q_x, q_y, q_d)):
+        share(q, c, slot).wait_send()
+        pair(q, slot).wait_send()
+    for step in range(1, n_z):
+        deliver(0, first, step).wait_send()
+        deliver(1, second, step).wait_send()
+    for block in range(n_z):
+        over_x(q_own, block).wait_send()
+        over_y(q_own, block).wait_send()
+        diag_x(q_y, block).wait_send()
+        diag_y(q_x, block).wait_send()
+        pl.when((z + 1 < n_z) & (block <= z))(lambda: along_z(block, True).wait_send())
+        pl.when((z >= 1) & (block >= z))(lambda: along_z(block, False).wait_send())
+
+
+def routed_experts(normed, hidden_state, w_gate_up, w_down, expert_ids, mix_weights):
+    n_z = lax.axis_size("ep") // 2
+    n_experts = lax.axis_size("ep") * lax.axis_size("tp")
+    rows, half = normed.shape
+    marks = expert_ids[:, :, None] == jnp.arange(n_experts, dtype=jnp.int32)
+    shares = jnp.sum(jnp.where(marks, mix_weights[:, :, None], 0.0), axis=1)
+    pieces, left = [], shares
+    for _ in range(3):
+        piece = lax.reduce_precision(left, 8, 7)
+        pieces.append(piece.astype(jnp.bfloat16))
+        left = left - piece
+    parts = len(pieces)
+    spare = -(parts * n_experts) % 128
+    pieces.append(jnp.zeros((rows, spare), jnp.bfloat16))
+    sent = jnp.concatenate([normed] + pieces, axis=1)
+    width = sent.shape[1]
+    many = n_z * rows
+    cut = half // 2
+    dma = pltpu.SemaphoreType.DMA
+    return pl.pallas_call(
+        functools.partial(moe_kernel, n_z, n_experts, parts),
+        out_shape=jax.ShapeDtypeStruct((rows, half), jnp.bfloat16),
+        in_specs=[pl.BlockSpec(memory_space=pltpu.VMEM)] * 2
+        + [pl.BlockSpec(memory_space=pl.ANY)] * 2,
+        out_specs=pl.BlockSpec(memory_space=pltpu.VMEM),
+        scratch_shapes=[
+            pltpu.VMEM((4, 2, n_z, rows, width), jnp.bfloat16),
+            pltpu.VMEM(w_gate_up.shape[1:], jnp.bfloat16),
+            pltpu.VMEM(w_down.shape[1:], jnp.bfloat16),
+            pltpu.VMEM((4, 2, many, half), jnp.bfloat16),
+            pltpu.VMEM((4, many, half), jnp.bfloat16),
+            pltpu.VMEM((many, cut), jnp.bfloat16),
+            pltpu.VMEM((many, cut), jnp.bfloat16),
+            pltpu.VMEM((2, many, cut), jnp.bfloat16),
+            pltpu.VMEM((2, many, cut), jnp.bfloat16),
+            pltpu.VMEM((2, n_z - 1, rows, cut), jnp.bfloat16),
+            dma((2,)),
+            dma((2, n_z)),
+            dma((n_z,)),
+            dma((n_z,)),
+            dma((n_z,)),
+            dma((n_z,)),
+            dma((n_z,)),
+            dma((n_z,)),
+            dma((n_z,)),
+            dma((n_z,)),
+            dma((n_z,)),
+            dma((8,)),
+            dma((8,)),
+            dma((6,)),
+            dma((6,)),
+            dma((2, n_z - 1)),
+            dma((2, n_z - 1)),
+        ],
+        compiler_params=pltpu.CompilerParams(
+            collective_id=0, has_side_effects=True, vmem_limit_bytes=44 * 1024 * 1024
+        ),
+    )(sent, hidden_state, w_gate_up, w_down)
 
 
 def body(
@@ -101,6 +469,18 @@
     normed = (hidden_state * lax.rsqrt(squares / D + 1e-06)[:, None] * norm_gain[None, :]).astype(
         jnp.bfloat16
     )
+    if (
+        pool_size == 1
+        and tensor_size == 4
+        and context_size % 2 == 0
+        and context_size > 2
+        and w_gate_up.shape[0] == 1
+        and moe_rows % 16 == 0
+        and half % 1024 == 0
+    ):
+        return routed_experts(
+            normed, hidden_state, w_gate_up, w_down, expert_ids, mix_weights
+        )
     top_k = expert_ids.shape[1]
     local_experts = w_gate_up.shape[0]
     experts = local_experts * context_size * tensor_size

time: 225 us -> 154 us (0.68)
  Pallas kernels: 0 us -> 62.4 us
  blocking collectives: 88.5 us -> 33 us
  waiting for transfers between devices: 70.2 us -> 19.3 us
  matrix products: 20 us -> 9.03 us
  local copies, waits for them, and re-layouts: 16.9 us -> 9.01 us
  other arithmetic: 11.2 us -> 7.18 us
  starting transfers between devices: 3.79 us -> 0.01 us
    pallas_call x0 -> x1, Pallas kernels: none -> 62.4 us  [routed_experts(): pl.pallas_call(functools.partial(moe_kernel, n_z, n_experts, parts), out_...]
    all_to_all x1 -> x0, blocking collectives: 53.3 us -> none  [body(): lax.all_to_all(shaped, ('ep', 'tp'), split_axis=0, concat_axis=0, tiled=T...]
    all_to_all x1 -> x0, waiting for transfers between devices: 48.8 us -> none  [body(): lax.all_to_all(finished, ('ep', 'tp'), split_axis=0, concat_axis=0, tiled...]
    scatter x1 -> x0, local copies, waits for them, and re-layouts: 7.06 us -> none  [body(): jnp.zeros((experts * capacity, half), jnp.bfloat16).at[slot]]
    gather x1 -> x0, local copies, waits for them, and re-layouts: 5.24 us -> none  [body(): back_rows = back.reshape(experts * capacity, half)[slot]]
    dot_general x2, matrix products: 5.41 us -> 0.93 us  [one_block(): jnp.einsum('rhd,nd->hrn', query_heads, block[:, :HD], preferred_element_t...]
    dot_general x2 -> x0, matrix products: 4.37 us -> none  [the longest x1 2.57 us: body(): jnp.einsum('slcf,lfd->slcd', hidden, w_down, preferred_element_type=jnp.f...]
    unnamed x18 -> x15, local copies, waits for them, and re-layouts: 3.08 us -> 7.39 us
  transfers between devices with their start and end apart: 2 -> 1, of which waited for: 2 -> 1; matrix products, arithmetic and copies ran while one was open for 1% -> 2% of each run, Pallas kernels for 0% -> 0%
where the time goes in v1:
time: 154 us; the launch traced here: 153 us
  Pallas kernels  62.4 us (41%)
  blocking collectives  33 us (21%)
  waiting for transfers between devices  19.3 us (13%)
  between operations  13.4 us (9%)
  matrix products  9.03 us (6%)
  local copies, waits for them, and re-layouts  9.01 us (6%)
  other arithmetic  7.18 us (5%)
    pallas_call x1, Pallas kernels, routed_experts(): pl.pallas_call(functools.partial(moe_kernel, n_z, n_experts, parts), out_...  62.4 us
    all_gather x1, blocking collectives, body(): piece = lax.all_gather(own_pairs, 'ep', axis=0, tiled=True)  33 us
    reduce_scatter x1, waiting for transfers between devices, body(): lax.psum_scatter(jnp.concatenate(pieces, axis=0).astype(jnp.bfloat16), ('...  19.3 us
    unnamed x15, local copies, waits for them, and re-layouts  7.39 us
    dot_general x1, matrix products, body(): jnp.einsum('hrd,hde->re', attended, weights, preferred_element_type=jnp.f...  4.06 us
    dot_general x2, matrix products, one_block(): jnp.einsum('hrn,nd->hrd', weights.astype(jnp.bfloat16), block[:, HD:], pr...  4.04 us
  transfers between devices with their start and end apart: 1, of which 1 were waited for; matrix products, arithmetic and copies ran while one was open for 2% of the time, Pallas kernels for 0%

profile of v1, /device:TPU:0, one launch (start us, length us, event | category | flops | bytes accessed | tf_op | source)
XLA Modules:
  0.0 153.5 jit_solution(10829433900986208618)
XLA Ops:
  6.5 0.9 copy-done
  7.5 33.0 %all_gather.3 = bf16[1024,256]{1,0:T(8,128)(2,1)S(1)} all-gather(bf16[128,256]{1,0:T(8,128)(2,1)S(1)} %constant_dynamic-slice_fusion), channel_id=1, replica_groups=mesh['grp'=1,'pool'=1,'ep'=8,'tp'=4] {'ep'}, dimensions={0}, use_global_device_ids=true | all-gather | bytes 589824 | tf_op jit(solution)/shard_map/all_gather | solution.py:419
  40.5 0.8 broadcast_in_dim.103
  41.3 1.1 copy.20
  42.5 0.2 copy.21
  42.6 0.1 convert_reduce_fusion.1
  42.7 6.4 %while.20 = (s32[]{:T(128)}, f32[8,128]{1,0:T(8,128)S(1)}, f32[8,128]{1,0:T(8,128)S(1)}, f32[8,128,128]{2,1,0:T(8,128)}, s32[128]{0:T(128)S(1)}, /*index=5*/s32[...) while((s32[]{:T(128)}, f32[8,128]{1,0:T(8,128)S(1)}, ...), condition=%wide.region_6.7_spmd.clone, body=%wide.region_2.6_spmd.clone.sunk | while | flops 274671104 | bytes 8200927 | solution.py:448
  42.7 0.1 convert_reduce_fusion.3
  42.8 0.1 broadcast_compare_fusion.2
  43.0 0.5 fusion.28
  43.5 0.4 fusion.29
  43.9 1.5 convolution_add_fusion.2
  45.4 0.1 convert_reduce_fusion.3
  45.5 0.1 broadcast_compare_fusion.2
  45.7 0.5 fusion.28
  46.2 0.4 fusion.29
  46.6 2.5 %convolution_add_fusion.2 = f32[8,128,128]{2,1,0:T(8,128)} fusion(f32[512,128,8]{1,0,2:T(8,128)S(1)} %get-tuple-element.321, f32[8,128]{1,0:T(8,128)S(1)} %select_maximum_fusion.2, pred[128,512]{0,1:T(8,128)(4,1)S(1)} %broadcast_compare_fusion.2, f32[8,128,128]{2,1,0:T(8,128)} %get-tuple-element.340, f32[8,128]{1,0:T(8,128)S(1)} %get-tuple-element.323, ...), kind=kOutput, calls=%fused_computation.7.clone.1 | convolution fusion | flops 136708096 | bytes 3350537 | tf_op jit(solution)/shard_map/while/body/eval_jaxpr/hrn,nd->hrd/dot_general | solution.py:440
  49.2 4.1 %fusion.15 = bf16[128,2048]{1,0:T(8,128)(2,1)} fusion(bf16[8,128,2048]{2,1,0:T(8,128)(2,1)} %bitcast.50, f32[8,128,128]{2,1,0:T(8,128)} %get-tuple-element.197, f32[8,128]{1,0:T(8,128)S(1)} %get-tuple-element.198), kind=kOutput, calls=%fused_computation.27 | convolution fusion | flops 537395200 | bytes 5246976 | tf_op jit(solution)/shard_map/hrd,hde->re/dot_general | solution.py:459
  53.2 0.0 reduce-scatter.2.cloned.1.call-update
  53.2 0.8 copy.22
  54.0 1.4 copy.23
  55.4 0.9 select_reduce_fusion
  56.2 0.6 fusion.18
  56.8 19.3 %reduce-scatter.2.cloned.1.call-done = bf16[32,2048]{1,0:T(8,128)(2,1)} async-done(((bf16[128,2048]{1,0:T(8,128)(2,1)}), bf16[32,2048]{1,0:T(8,128)(2,1)}) %reduce-scatter.2.cloned.1.call-update) | async-done | bytes 131088 | tf_op jit(solution)/shard_map/reduce_scatter | solution.py:461
  76.2 1.7 %convert_add_fusion = (f32[32,2048]{1,0:T(8,128)}, f32[32]{0:T(128)S(1)}) fusion(bf16[32,2048]{1,0:T(8,128)(2,1)} %reduce-scatter.2.cloned.1.call-done, bf16[32,2048]{1,0:T(8,128)(2,1)S(1)} %copy-done.4), kind=kLoop, calls=%fused_computation.31 | loop fusion | flops 327648 | bytes 524416 | tf_op jit(solution)/shard_map/add | solution.py:467
  77.9 1.7 %multiply_convert_fusion = bf16[32,2048]{1,0:T(8,128)(2,1)} fusion(f32[2048]{0:T(1024)} %param.15, f32[32]{0:T(128)S(1)} %add_rsqrt_fusion, bf16[32,2048]{1,0:T(8,128)(2,1)} %reduce-scatter.2.cloned.1.call-done, bf16[32,2048]{1,0:T(8,128)(2,1)S(1)} %copy-done.4), kind=kLoop, calls=%fused_computation.29 | loop fusion | flops 393216 | bytes 401536 | tf_op jit(solution)/shard_map/convert_element_type | solution.py:469
  79.6 0.6 broadcast_in_dim.106
  80.2 1.0 concatenate.3.send_ref
  81.2 1.4 copy-done.2
  82.6 0.9 copy-done.3
  83.6 62.4 %shard_map.100 = bf16[32,2048]{1,0:T(8,128)(2,1)S(1)} custom-call(bf16[32,2176]{1,0:T(8,128)(2,1)S(1)} %concatenate.3.send_ref, f32[32,2048]{1,0:T(8,128)S(1)} %copy-done.3, bf16[1,2048,768]{2,1,0:T(8,128)(2,1)S(1)} %copy-done.1, bf16[1,384,2048]{2,1,0:T(8,128)(2,1)S(1)} %copy-done.2), custom_call_target="tpu_custom_call" | custom-call | tf_op jit(solution)/shard_map/pallas_call | solution.py:344
  146.0 0.7 copy.38
  (22 shorter events, 0.1 us)
Async XLA Ops:
  6.5 1.0 copy-start
  6.5 69.6 %reduce-scatter.2.cloned.1.call-start = ((), (), s32[]{:S(2)}) async-start(), calls=%async_computation.1 | async-start | bytes 655360 | tf_op jit(solution)/shard_map/reduce_scatter | solution.py:461
  49.2 27.0 %copy-start.4 = (bf16[32,2048]{1,0:T(8,128)(2,1)S(1)}, bf16[32,2048]{1,0:T(8,128)(2,1)}, u32[]{:S(2)}) copy-start(bf16[32,2048]{1,0:T(8,128)(2,1)} %param.14) | copy-start | bytes 393220
  49.2 32.1 %copy-start.1 = (bf16[1,2048,768]{2,1,0:T(8,128)(2,1)S(1)}, bf16[1,2048,768]{2,1,0:T(8,128)(2,1)}, u32[]{:S(2)}) copy-start(bf16[1,2048,768]{2,1,0:T(8,128)(2,1)} %wgu_hbm.1) | copy-start | bytes 9437188
  81.2 1.4 copy-start.2
  82.6 0.9 copy-start.3
Sparse Core Ops, SparseCore 0:
  53.4 22.7 reduce-scatter.1

commit v2 on v1

--- a/solution.py
+++ b/solution.py
@@ -18,15 +18,34 @@
     return jnp.sum((places[:, None] >= ends[None, :]).astype(jnp.int32), axis=1)
 
 
-def moe_kernel(
+def layer_kernel(
     n_z,
     n_experts,
     parts,
-    send_ref,
-    hidden_ref,
+    clip_ref,
+    queries_ref,
+    kv_ref,
+    residual_ref,
+    gain_ref,
+    ids_ref,
+    mix_ref,
+    wo_hbm,
     wgu_hbm,
     wd_hbm,
     out_ref,
+    kv,
+    attended,
+    proj,
+    sib_in,
+    x_in,
+    hidden_ref,
+    wo,
+    kz_send,
+    kz_recv,
+    ky_send,
+    ky_recv,
+    at_send,
+    at_recv,
     held,
     wgu,
     wd,
@@ -59,10 +78,11 @@
     tp = lax.axis_index("tp")
     z, y = ep // 2, ep % 2
     x, c = tp // 2, tp % 2
-    rows = send_ref.shape[0]
-    half = hidden_ref.shape[1]
+    rows, half = residual_ref.shape
     cut = half // 2
-    width = send_ref.shape[1]
+    quarter = half // 4
+    width = held.shape[4]
+    q_rows = queries_ref.shape[0]
     first, second, rest = pl.ds(0, cut), pl.ds(cut, cut), pl.ds(cut, width - cut)
     x_peer = (ep, (1 - x) * 2 + c)
     y_peer = (z * 2 + 1 - y, tp)
@@ -70,8 +90,10 @@
     q_own, q_x = x * 2 + y, (1 - x) * 2 + y
     q_y, q_d = x * 2 + 1 - y, (1 - x) * 2 + 1 - y
 
+    load_o = pltpu.make_async_copy(wo_hbm, wo, w_sem.at[2])
     load_gu = pltpu.make_async_copy(wgu_hbm.at[0], wgu, w_sem.at[0])
     load_d = pltpu.make_async_copy(wd_hbm.at[0], wd, w_sem.at[1])
+    load_o.start()
     load_gu.start()
     load_d.start()
 
@@ -131,15 +153,148 @@
         here = held.at[q, core]
         return remote(here, here, sib_send.at[slot], sib_recv.at[slot], sib)
 
-    held[q_own, c, z] = send_ref[...]
-    pl.semaphore_wait(barrier, 3 + n_z - 1)
-
     def each_at(distance, act):
         if distance == 0:
             act(z, 0)
             return
         pl.when(z - distance >= 0)(lambda: act(z - distance, -1))
         pl.when(z + distance < n_z)(lambda: act(z + distance, 1))
+
+    def keys_z(block, up):
+        there = z + 1 if up else z - 1
+        here = kv.at[block * 2 + y]
+        return remote(
+            here, here, kz_send.at[1 if up else 0, block], kz_recv.at[block], (there * 2 + y, tp)
+        )
+
+    def keys_y(block, side_y):
+        here = kv.at[block * 2 + side_y]
+        return remote(here, here, ky_send.at[block], ky_recv.at[block], y_peer)
+
+    def keys_arrive(block, side):
+        if side:
+            keys_z(block, side < 0).wait_recv()
+        if side <= 0:
+            pl.when(z + 1 < n_z)(lambda: keys_z(block, True).start())
+        if side >= 0:
+            pl.when(z >= 1)(lambda: keys_z(block, False).start())
+        keys_y(block, y).start()
+
+    pair_width = kv.shape[2]
+    head = pair_width // 2
+    kv[ep] = kv_ref[:, pl.ds(pl.multiple_of(tp * pair_width, pair_width), pair_width)]
+    pl.semaphore_wait(barrier, 3 + n_z - 1)
+    for distance in range(n_z):
+        each_at(distance, keys_arrive)
+
+    n_keys = 2 * n_z * q_rows
+    place = lax.broadcasted_iota(jnp.int32, (2 * q_rows, 1), 0)
+    place = jnp.where(place >= q_rows, place - q_rows, place) + ep * q_rows
+    key_place = lax.broadcasted_iota(jnp.int32, (1, n_keys), 1)
+    clip = jnp.zeros(place.shape, jnp.int32)
+    key_clip = jnp.zeros(key_place.shape, jnp.int32)
+    end = jnp.int32(0)
+    for number in range(clip_ref.shape[0]):
+        end = end + clip_ref[number]
+        clip = clip + jnp.where(place >= end, 1, 0)
+        key_clip = key_clip + jnp.where(key_place >= end, 1, 0)
+    same = clip == key_clip
+
+    lane = lax.broadcasted_iota(jnp.int32, (rows, width - half), 1)
+    base = jnp.zeros(lane.shape, jnp.int32)
+    for part in range(1, parts):
+        base = base + jnp.where(lane >= part * n_experts, n_experts, 0)
+    wanted = lane - base
+    weight = jnp.zeros(lane.shape, jnp.float32)
+    for slot in range(ids_ref.shape[1]):
+        weight = weight + jnp.where(
+            ids_ref[:, slot : slot + 1] == wanted, mix_ref[:, slot : slot + 1], 0.0
+        )
+    packed = jnp.zeros(lane.shape, jnp.float32)
+    for part in range(parts):
+        piece = weight.astype(jnp.bfloat16).astype(jnp.float32)
+        packed = jnp.where(base == part * n_experts, piece, packed)
+        weight = weight - piece
+    held[q_own, c, z, :, half:width] = packed.astype(jnp.bfloat16)
+
+    for block in range(n_z):
+        keys_y(block, 1 - y).wait_recv()
+    keys = kv[:, :, 0:head].reshape(n_keys, head)
+    values = kv[:, :, head:pair_width].reshape(n_keys, head)
+    scale = head ** (-0.5)
+    for at in range(0, queries_ref.shape[1], 2 * head):
+        two = jnp.concatenate(
+            [queries_ref[:, at : at + head], queries_ref[:, at + head : at + 2 * head]], axis=0
+        )
+        scores = lax.dot_general(
+            two, keys, (((1,), (1,)), ((), ())), preferred_element_type=jnp.float32
+        )
+        scores = jnp.where(same, scores * scale, -1e30)
+        top = jnp.max(scores, axis=1, keepdims=True)
+        weights = jnp.exp(scores - top)
+        total = jnp.sum(weights, axis=1, keepdims=True)
+        numer = jnp.dot(
+            weights.astype(jnp.bfloat16), values, preferred_element_type=jnp.float32
+        )
+        result = (numer / total).astype(jnp.bfloat16)
+        attended[:, at : at + head] = result[0:q_rows]
+        attended[:, at + head : at + 2 * head] = result[q_rows : 2 * q_rows]
+
+    def proj_pair(part):
+        columns = pl.ds(part * cut, cut)
+        return remote(
+            proj.at[1 - c, :, :, columns],
+            sib_in.at[:, :, columns],
+            at_send.at[part],
+            at_recv.at[part],
+            sib,
+        )
+
+    def proj_x(part):
+        columns = pl.ds(part * cut, cut)
+        return remote(
+            proj.at[c, 1 - x, :, columns],
+            x_in.at[:, columns],
+            at_send.at[2 + part],
+            at_recv.at[2 + part],
+            x_peer,
+        )
+
+    load_o.wait()
+    for part in range(2):
+        for at in range(part * cut, (part + 1) * cut, quarter):
+            result = jnp.dot(
+                attended[...], wo[:, at : at + quarter], preferred_element_type=jnp.float32
+            ).astype(jnp.bfloat16)
+            for side_x in range(2):
+                for side_c in range(2):
+                    start = (side_x * 2 + side_c) * rows
+                    proj[side_c, side_x, :, at : at + quarter] = result[start : start + rows]
+        proj_pair(part).start()
+    for part in range(2):
+        columns = pl.ds(part * cut, cut)
+        proj_pair(part).wait_recv()
+        proj[c, 1 - x, :, columns] = (
+            proj[c, 1 - x, :, columns].astype(jnp.float32)
+            + sib_in[1 - x, :, columns].astype(jnp.float32)
+        ).astype(jnp.bfloat16)
+        proj_x(part).start()
+    for part in range(2):
+        columns = pl.ds(part * cut, cut)
+        hidden_ref[:, columns] = (
+            residual_ref[:, columns].astype(jnp.float32)
+            + proj[c, x, :, columns].astype(jnp.float32)
+            + sib_in[x, :, columns].astype(jnp.float32)
+        )
+    for part in range(2):
+        columns = pl.ds(part * cut, cut)
+        proj_x(part).wait_recv()
+        hidden_ref[:, columns] += x_in[:, columns].astype(jnp.float32)
+    hidden = hidden_ref[...]
+    squares = jnp.sum(hidden * hidden, axis=1, keepdims=True) / half
+    held[q_own, c, z, :, 0:half] = (hidden * lax.rsqrt(squares + 1e-06) * gain_ref[...]).astype(
+        jnp.bfloat16
+    )
 
     def arrive_z(block, side):
         if side:
@@ -217,12 +372,14 @@
     def reduce_y(q, columns, into, slot):
         return remote(term.at[q, c, :, columns], into, r_send.at[slot], r_recv.at[slot], y_peer)
 
+    low = [pl.ds(0, quarter), pl.ds(quarter, quarter)]
+    high = [pl.ds(cut, quarter), pl.ds(cut + quarter, quarter)]
     own_x = reduce_x(q_x, first, from_x.at[0], 0)
     own_y = reduce_y(q_y, second, from_y.at[1], 1)
-    pass_x = reduce_x(q_d, first, relay_x, 2)
-    pass_y = reduce_y(q_d, second, relay_y, 3)
-    last_x = reduce_x(q_x, second, from_x.at[1], 4)
-    last_y = reduce_y(q_y, first, from_y.at[0], 5)
+    pass_x = [reduce_x(q_d, low[i], relay_x.at[:, low[i]], 2 + i) for i in range(2)]
+    pass_y = [reduce_y(q_d, high[i], relay_y.at[:, low[i]], 4 + i) for i in range(2)]
+    last_x = [reduce_x(q_x, high[i], from_x.at[1, :, low[i]], 6 + i) for i in range(2)]
+    last_y = [reduce_y(q_y, low[i], from_y.at[0, :, low[i]], 8 + i) for i in range(2)]
 
     share(q_own, 1 - c, 0).wait_recv()
     compute(q_own)
@@ -245,75 +402,84 @@
     add_pair(q_y, 2)
     own_y.start()
     add_pair(q_d, 3)
-    pass_x.start()
-    pass_y.start()
+    for i in range(2):
+        pass_x[i].start()
+        pass_y[i].start()
     add_pair(q_own, 0)
 
-    pass_x.wait_recv()
-    term[q_y, c, :, first] = (
-        term[q_y, c, :, first].astype(jnp.float32) + relay_x[...].astype(jnp.float32)
-    ).astype(jnp.bfloat16)
-    last_y.start()
-    pass_y.wait_recv()
-    term[q_x, c, :, second] = (
-        term[q_x, c, :, second].astype(jnp.float32) + relay_y[...].astype(jnp.float32)
-    ).astype(jnp.bfloat16)
-    last_x.start()
-
-    def finish(number, columns):
+    for i in range(2):
+        pass_x[i].wait_recv()
+        term[q_y, c, :, low[i]] = (
+            term[q_y, c, :, low[i]].astype(jnp.float32) + relay_x[:, low[i]].astype(jnp.float32)
+        ).astype(jnp.bfloat16)
+        last_y[i].start()
+        pass_y[i].wait_recv()
+        term[q_x, c, :, high[i]] = (
+            term[q_x, c, :, high[i]].astype(jnp.float32) + relay_y[:, low[i]].astype(jnp.float32)
+        ).astype(jnp.bfloat16)
+        last_x[i].start()
+
+    def finish(side, i):
+        columns = high[i] if side else low[i]
         term[q_own, c, :, columns] = (
             term[q_own, c, :, columns].astype(jnp.float32)
-            + from_x[number].astype(jnp.float32)
-            + from_y[number].astype(jnp.float32)
+            + from_x[side, :, low[i]].astype(jnp.float32)
+            + from_y[side, :, low[i]].astype(jnp.float32)
         ).astype(jnp.bfloat16)
 
-    def deliver(number, columns, step):
+    def deliver(side, i, step):
         there = (z + step) % n_z
         return remote(
-            term.at[q_own, c, pl.ds(pl.multiple_of(there * rows, rows), rows), columns],
-            from_z.at[number, n_z - 1 - step],
-            rz_send.at[number, step - 1],
-            rz_recv.at[number, n_z - 1 - step],
+            term.at[
+                q_own,
+                c,
+                pl.ds(pl.multiple_of(there * rows, rows), rows),
+                high[i] if side else low[i],
+            ],
+            from_z.at[side, i, n_z - 1 - step],
+            rz_send.at[side, i, step - 1],
+            rz_recv.at[side, i, n_z - 1 - step],
             (there * 2 + y, tp),
         )
 
-    def collect(number, columns):
+    def collect(side, i):
+        columns = high[i] if side else low[i]
         total = hidden_ref[:, columns] + term[
             q_own, c, pl.ds(pl.multiple_of(z * rows, rows), rows), columns
         ].astype(jnp.float32)
-        for slot in range(n_z - 1):
-            remote(
-                from_z.at[number, slot],
-                from_z.at[number, slot],
-                rz_send.at[number, slot],
-                rz_recv.at[number, slot],
-                sib,
-            ).wait_recv()
-            total = total + from_z[number, slot].astype(jnp.float32)
+        for step in range(1, n_z):
+            deliver(side, i, step).wait_recv()
+            total = total + from_z[side, i, n_z - 1 - step].astype(jnp.float32)
         out_ref[:, columns] = total.astype(jnp.bfloat16)
 
     own_x.wait_recv()
-    last_y.wait_recv()
-    finish(0, first)
-    for step in range(1, n_z):
-        deliver(0, first, step).start()
     own_y.wait_recv()
-    last_x.wait_recv()
-    finish(1, second)
-    for step in range(1, n_z):
-        deliver(1, second, step).start()
-    collect(0, first)
-    collect(1, second)
-
-    for copy in (own_x, own_y, pass_x, pass_y, last_x, last_y):
+    for i in range(2):
+        for side in range(2):
+            (last_x if side else last_y)[i].wait_recv()
+            finish(side, i)
+            for step in range(1, n_z):
+                deliver(side, i, step).start()
+    for i in range(2):
+        for side in range(2):
+            collect(side, i)
+
+    for copy in [own_x, own_y] + pass_x + pass_y + last_x + last_y:
         copy.wait_send()
+    for part in range(2):
+        proj_pair(part).wait_send()
+        proj_x(part).wait_send()
     for slot, q in enumerate((q_own, q_x, q_y, q_d)):
         share(q, c, slot).wait_send()
         pair(q, slot).wait_send()
     for step in range(1, n_z):
-        deliver(0, first, step).wait_send()
-        deliver(1, second, step).wait_send()
+        for i in range(2):
+            for side in range(2):
+                deliver(side, i, step).wait_send()
     for block in range(n_z):
+        keys_y(block, y).wait_send()
+        pl.when((z + 1 < n_z) & (block <= z))(lambda: keys_z(block, True).wait_send())
+        pl.when((z >= 1) & (block >= z))(lambda: keys_z(block, False).wait_send())
         over_x(q_own, block).wait_send()
         over_y(q_own, block).wait_send()
         diag_x(q_y, block).wait_send()
@@ -322,64 +488,83 @@
         pl.when((z >= 1) & (block >= z))(lambda: along_z(block, False).wait_send())
 
 
-def routed_experts(normed, hidden_state, w_gate_up, w_down, expert_ids, mix_weights):
-    n_z = lax.axis_size("ep") // 2
-    n_experts = lax.axis_size("ep") * lax.axis_size("tp")
-    rows, half = normed.shape
-    marks = expert_ids[:, :, None] == jnp.arange(n_experts, dtype=jnp.int32)
-    shares = jnp.sum(jnp.where(marks, mix_weights[:, :, None], 0.0), axis=1)
-    pieces, left = [], shares
-    for _ in range(3):
-        piece = lax.reduce_precision(left, 8, 7)
-        pieces.append(piece.astype(jnp.bfloat16))
-        left = left - piece
-    parts = len(pieces)
-    spare = -(parts * n_experts) % 128
-    pieces.append(jnp.zeros((rows, spare), jnp.bfloat16))
-    sent = jnp.concatenate([normed] + pieces, axis=1)
-    width = sent.shape[1]
+def whole_layer(
+    queries,
+    keys_values,
+    residual,
+    norm_gain,
+    w_out,
+    w_gate_up,
+    w_down,
+    expert_ids,
+    mix_weights,
+    clip_lengths,
+):
+    n_ep = lax.axis_size("ep")
+    n_z = n_ep // 2
+    n_experts = n_ep * lax.axis_size("tp")
+    rows, half = residual.shape
+    q_rows = queries.shape[0]
+    parts = 3
+    width = half + -(-parts * n_experts // 128) * 128
     many = n_z * rows
     cut = half // 2
     dma = pltpu.SemaphoreType.DMA
+    bf16 = jnp.bfloat16
+    in_vmem = pl.BlockSpec(memory_space=pltpu.VMEM)
     return pl.pallas_call(
-        functools.partial(moe_kernel, n_z, n_experts, parts),
-        out_shape=jax.ShapeDtypeStruct((rows, half), jnp.bfloat16),
-        in_specs=[pl.BlockSpec(memory_space=pltpu.VMEM)] * 2
-        + [pl.BlockSpec(memory_space=pl.ANY)] * 2,
-        out_specs=pl.BlockSpec(memory_space=pltpu.VMEM),
+        functools.partial(layer_kernel, n_z, n_experts, parts),
+        out_shape=jax.ShapeDtypeStruct((rows, half), bf16),
+        in_specs=[pl.BlockSpec(memory_space=pltpu.SMEM)]
+        + [in_vmem] * 6
+        + [pl.BlockSpec(memory_space=pl.ANY)] * 3,
+        out_specs=in_vmem,
         scratch_shapes=[
-            pltpu.VMEM((4, 2, n_z, rows, width), jnp.bfloat16),
-            pltpu.VMEM(w_gate_up.shape[1:], jnp.bfloat16),
-            pltpu.VMEM(w_down.shape[1:], jnp.bfloat16),
-            pltpu.VMEM((4, 2, many, half), jnp.bfloat16),
-            pltpu.VMEM((4, many, half), jnp.bfloat16),
-            pltpu.VMEM((many, cut), jnp.bfloat16),
-            pltpu.VMEM((many, cut), jnp.bfloat16),
-            pltpu.VMEM((2, many, cut), jnp.bfloat16),
-            pltpu.VMEM((2, many, cut), jnp.bfloat16),
-            pltpu.VMEM((2, n_z - 1, rows, cut), jnp.bfloat16),
-            dma((2,)),
+            pltpu.VMEM((n_ep, q_rows, 2 * HD), bf16),
+            pltpu.VMEM(queries.shape, bf16),
+            pltpu.VMEM((2, 2, rows, half), bf16),
+            pltpu.VMEM((2, rows, half), bf16),
+            pltpu.VMEM((rows, half), bf16),
+            pltpu.VMEM((rows, half), jnp.float32),
+            pltpu.VMEM(w_out.shape, bf16),
             dma((2, n_z)),
             dma((n_z,)),
             dma((n_z,)),
             dma((n_z,)),
-            dma((n_z,)),
-            dma((n_z,)),
-            dma((n_z,)),
-            dma((n_z,)),
-            dma((n_z,)),
-            dma((n_z,)),
-            dma((8,)),
-            dma((8,)),
-            dma((6,)),
-            dma((6,)),
-            dma((2, n_z - 1)),
-            dma((2, n_z - 1)),
-        ],
+            dma((4,)),
+            dma((4,)),
+            pltpu.VMEM((4, 2, n_z, rows, width), bf16),
+            pltpu.VMEM(w_gate_up.shape[1:], bf16),
+            pltpu.VMEM(w_down.shape[1:], bf16),
+            pltpu.VMEM((4, 2, many, half), bf16),
+            pltpu.VMEM((4, many, half), bf16),
+            pltpu.VMEM((many, cut), bf16),
+            pltpu.VMEM((many, cut), bf16),
+            pltpu.VMEM((2, many, cut), bf16),
+            pltpu.VMEM((2, many, cut), bf16),
+            pltpu.VMEM((2, 2, n_z - 1, rows, cut // 2), bf16),
+            dma((3,)),
+            dma((2, n_z)),
+        ]
+        + [dma((n_z,))] * 9
+        + [dma((8,))] * 2
+        + [dma((10,))] * 2
+        + [dma((2, 2, n_z - 1))] * 2,
         compiler_params=pltpu.CompilerParams(
-            collective_id=0, has_side_effects=True, vmem_limit_bytes=44 * 1024 * 1024
+            collective_id=0, has_side_effects=True, vmem_limit_bytes=48 * 1024 * 1024
         ),
-    )(sent, hidden_state, w_gate_up, w_down)
+    )(
+        clip_lengths,
+        queries,
+        keys_values,
+        residual,
+        norm_gain.reshape(1, half),
+        expert_ids,
+        mix_weights,
+        w_out,
+        w_gate_up,
+        w_down,
+    )
 
 
 def body(
@@ -396,6 +581,29 @@
 ):
     rows = queries.shape[0]
     heads_here = queries.shape[1] // HD
+    if (
+        lax.axis_size("pool") == 1
+        and lax.axis_size("tp") == 4
+        and lax.axis_size("ep") % 2 == 0
+        and lax.axis_size("ep") > 2
+        and heads_here == QH // KVH
+        and w_gate_up.shape[0] == 1
+        and residual.shape[0] % 16 == 0
+        and residual.shape[1] == D
+        and rows == 4 * residual.shape[0]
+    ):
+        return whole_layer(
+            queries,
+            keys_values,
+            residual,
+            norm_gain,
+            w_out,
+            w_gate_up,
+            w_down,
+            expert_ids,
+            mix_weights,
+            clip_lengths,
+        )
     pool_size = lax.axis_size("pool")
     tensor_size = lax.axis_size("tp")
     context_size = lax.axis_size("ep")
@@ -469,18 +677,6 @@
     normed = (hidden_state * lax.rsqrt(squares / D + 1e-06)[:, None] * norm_gain[None, :]).astype(
         jnp.bfloat16
     )
-    if (
-        pool_size == 1
-        and tensor_size == 4
-        and context_size % 2 == 0
-        and context_size > 2
-        and w_gate_up.shape[0] == 1
-        and moe_rows % 16 == 0
-        and half % 1024 == 0
-    ):
-        return routed_experts(
-            normed, hidden_state, w_gate_up, w_down, expert_ids, mix_weights
-        )
     top_k = expert_ids.shape[1]
     local_experts = w_gate_up.shape[0]
     experts = local_experts * context_size * tensor_size

time: 154 us -> 94.1 us (0.61)
  blocking collectives: 33 us -> 0 us
  Pallas kernels: 62.4 us -> 84.1 us
  waiting for transfers between devices: 19.3 us -> 0 us
  between operations: 13.4 us -> 0.02 us
  matrix products: 9.03 us -> 0 us
  other arithmetic: 7.18 us -> 0 us
    all_gather x1 -> x0, blocking collectives: 33 us -> none  [body(): piece = lax.all_gather(own_pairs, 'ep', axis=0, tiled=True)]
    pallas_call x1, Pallas kernels: 62.4 us -> 84.1 us  [whole_layer(): pl.pallas_call(functools.partial(layer_kernel, n_z, n_experts, parts), ou...]
    reduce_scatter x1 -> x0, waiting for transfers between devices: 19.3 us -> none  [body(): lax.psum_scatter(jnp.concatenate(pieces, axis=0).astype(jnp.bfloat16), ('...]
    dot_general x5 -> x0, matrix products: 9.03 us -> none  [the longest x1 4.06 us: body(): jnp.einsum('hrd,hde->re', attended, weights, preferred_element_type=jnp.f...]
    convert_element_type x2 -> x0, other arithmetic: 2.28 us -> none  [the longest x1 1.68 us: body(): (hidden_state * lax.rsqrt(squares / D + 1e-06)[:, None] * norm_gain[None,...]
    unnamed x15 -> x17, local copies, waits for them, and re-layouts: 7.39 us -> 9.63 us
    reduce_sum x6 -> x0, other arithmetic: 2 us -> none  [the longest x2 0.88 us: one_block(): total = total * factor + jnp.sum(weights, axis=2)]
    add x6 -> x0, other arithmetic: 1.78 us -> none  [the longest x1 1.74 us: body(): hidden_state = residual.astype(jnp.float32) + mixed]
  transfers between devices with their start and end apart: 1 -> 0, of which waited for: 1 -> 0; matrix products, arithmetic and copies ran while one was open for 2% -> 0% of each run, Pallas kernels for 0% -> 0%
where the time goes in v2:
time: 94.1 us; the launch traced here: 93.7 us
  Pallas kernels  84.1 us (89%)
  local copies, waits for them, and re-layouts  9.63 us (10%)
    pallas_call x1, Pallas kernels, whole_layer(): pl.pallas_call(functools.partial(layer_kernel, n_z, n_experts, parts), ou...  84.1 us
    unnamed x17, local copies, waits for them, and re-layouts  9.63 us

profile of v2, /device:TPU:0, one launch (start us, length us, event | category | flops | bytes accessed | tf_op | source)
XLA Modules:
  0.0 93.7 jit_solution(3435218819069141313)
XLA Ops:
  0.0 0.8 copy.11.ids_ref
  0.8 0.8 copy.12.mix_ref
  1.5 0.0 copy-start
  1.5 1.9 %copy-done = bf16[1,2048,768]{2,1,0:T(8,128)(2,1)S(1)} copy-done((bf16[1,2048,768]{2,1,0:T(8,128)(2,1)S(1)}, bf16[1,2048,768]{2,1,0:T(8,128)(2,1)}, u32[]{:S(2)}) %copy-start) | copy-done | bytes 3145752
  3.4 0.0 copy-start.1
  3.4 1.4 %copy-done.1 = bf16[1,384,2048]{2,1,0:T(8,128)(2,1)S(1)} copy-done((bf16[1,384,2048]{2,1,0:T(8,128)(2,1)S(1)}, bf16[1,384,2048]{2,1,0:T(8,128)(2,1)}, u32[]{:S(2)}) %copy-start.1) | copy-done | bytes 1572888
  4.8 0.0 copy-start.2
  4.8 0.9 %copy-done.2 = bf16[128,1024]{1,0:T(8,128)(2,1)S(1)} copy-done((bf16[128,1024]{1,0:T(8,128)(2,1)S(1)}, bf16[128,1024]{1,0:T(8,128)(2,1)}, u32[]{:S(2)}) %copy-start.2) | copy-done | bytes 262168
  5.8 0.0 copy-start.3
  5.8 0.9 %copy-done.3 = bf16[128,1024]{1,0:T(8,128)(2,1)S(1)} copy-done((bf16[128,1024]{1,0:T(8,128)(2,1)S(1)}, bf16[128,1024]{1,0:T(8,128)(2,1)}, u32[]{:S(2)}) %copy-start.3) | copy-done | bytes 262168
  6.7 0.0 copy-start.4
  6.7 0.9 copy-done.4
  7.6 0.0 copy-start.5
  7.6 0.7 copy-done.5
  8.3 0.0 copy-start.6
  8.3 0.7 copy-done.6
  9.0 84.1 %shard_map.100 = bf16[32,2048]{1,0:T(8,128)(2,1)S(1)} custom-call(s32[3]{0:T(128)S(1)} %copy-done.6, bf16[128,1024]{1,0:T(8,128)(2,1)S(1)} %copy-done.2, bf16[128,1024]{1,0:T(8,128)(2,1)S(1)} %copy-done.3, bf16[32,2048]{1,0:T(8,128)(2,1)S(1)} %copy-done.4, f32[1,2048]{1,0:T(1,128)S(1)} %bitcast.1, s32[32,8]{1,0:T(8,128)S(1)} %copy.11.ids_ref, ...), custom_call_target="tpu_custom_call" | custom-call | tf_op jit(solution)/shard_map/pallas_call | solution.py:515
  93.0 0.7 copy.14
Async XLA Ops:
  1.5 1.9 %copy-start = (bf16[1,2048,768]{2,1,0:T(8,128)(2,1)S(1)}, bf16[1,2048,768]{2,1,0:T(8,128)(2,1)}, u32[]{:S(2)}) copy-start(bf16[1,2048,768]{2,1,0:T(8,128)(2,1)} %wgu_hbm.1) | copy-start | bytes 9437188
  3.4 1.4 %copy-start.1 = (bf16[1,384,2048]{2,1,0:T(8,128)(2,1)S(1)}, bf16[1,384,2048]{2,1,0:T(8,128)(2,1)}, u32[]{:S(2)}) copy-start(bf16[1,384,2048]{2,1,0:T(8,128)(2,1)} %wd_hbm.1) | copy-start | bytes 4718596
  4.8 0.9 %copy-start.2 = (bf16[128,1024]{1,0:T(8,128)(2,1)S(1)}, bf16[128,1024]{1,0:T(8,128)(2,1)}, u32[]{:S(2)}) copy-start(bf16[128,1024]{1,0:T(8,128)(2,1)} %queries_ref.1) | copy-start | bytes 786436
  5.8 0.9 %copy-start.3 = (bf16[128,1024]{1,0:T(8,128)(2,1)S(1)}, bf16[128,1024]{1,0:T(8,128)(2,1)}, u32[]{:S(2)}) copy-start(bf16[128,1024]{1,0:T(8,128)(2,1)} %kv_ref.1) | copy-start | bytes 786436
  6.7 0.9 copy-start.4
  7.6 0.7 copy-start.5
  8.3 0.7 copy-start.6

commit v3 on v2

--- a/solution.py
+++ b/solution.py
@@ -1,4 +1,5 @@
 import functools
+import math
 
 import jax
 import jax.numpy as jnp
@@ -23,16 +24,21 @@
     n_experts,
     parts,
     clip_ref,
+    queries_hbm,
+    kv_hbm,
+    residual_hbm,
+    gain_hbm,
+    ids_hbm,
+    mix_hbm,
+    wo_hbm,
+    wgu_hbm,
+    wd_hbm,
+    out_ref,
     queries_ref,
-    kv_ref,
     residual_ref,
     gain_ref,
     ids_ref,
     mix_ref,
-    wo_hbm,
-    wgu_hbm,
-    wd_hbm,
-    out_ref,
     kv,
     attended,
     proj,
@@ -69,6 +75,8 @@
     db_recv,
     sib_send,
     sib_recv,
+    pair_send,
+    pair_recv,
     r_send,
     r_recv,
     rz_send,
@@ -90,12 +98,26 @@
     q_own, q_x = x * 2 + y, (1 - x) * 2 + y
     q_y, q_d = x * 2 + 1 - y, (1 - x) * 2 + 1 - y
 
-    load_o = pltpu.make_async_copy(wo_hbm, wo, w_sem.at[2])
-    load_gu = pltpu.make_async_copy(wgu_hbm.at[0], wgu, w_sem.at[0])
-    load_d = pltpu.make_async_copy(wd_hbm.at[0], wd, w_sem.at[1])
-    load_o.start()
-    load_gu.start()
-    load_d.start()
+    pair_width = kv.shape[2]
+    own_keys = kv_hbm.at[:, pl.ds(pl.multiple_of(tp * pair_width, pair_width), pair_width)]
+    loads = [
+        pltpu.make_async_copy(src, dst, w_sem.at[number])
+        for number, (src, dst) in enumerate(
+            (
+                (own_keys, kv.at[ep]),
+                (queries_hbm, queries_ref),
+                (ids_hbm, ids_ref),
+                (mix_hbm, mix_ref),
+                (residual_hbm, residual_ref),
+                (gain_hbm, gain_ref),
+                (wo_hbm, wo),
+                (wgu_hbm.at[0], wgu),
+                (wd_hbm.at[0], wd),
+            )
+        )
+    ]
+    for load in loads:
+        load.start()
 
     barrier = pltpu.get_barrier_semaphore()
     for peer in (x_peer, y_peer, sib):
@@ -149,9 +171,13 @@
         here = held.at[q, c, block, :, rest]
         return remote(here, here, db_send.at[block], db_recv.at[block], y_peer)
 
-    def share(q, core, slot):
-        here = held.at[q, core]
-        return remote(here, here, sib_send.at[slot], sib_recv.at[slot], sib)
+    def share(q, core, slot, block):
+        here = held.at[q, core, block]
+        return remote(here, here, sib_send.at[slot, block], sib_recv.at[slot, block], sib)
+
+    def shares_arrive(q, slot):
+        for block in range(n_z):
+            share(q, 1 - c, slot, block).wait_recv()
 
     def each_at(distance, act):
         if distance == 0:
@@ -180,9 +206,8 @@
             pl.when(z >= 1)(lambda: keys_z(block, False).start())
         keys_y(block, y).start()
 
-    pair_width = kv.shape[2]
     head = pair_width // 2
-    kv[ep] = kv_ref[:, pl.ds(pl.multiple_of(tp * pair_width, pair_width), pair_width)]
+    loads[0].wait()
     pl.semaphore_wait(barrier, 3 + n_z - 1)
     for distance in range(n_z):
         each_at(distance, keys_arrive)
@@ -200,28 +225,39 @@
         key_clip = key_clip + jnp.where(key_place >= end, 1, 0)
     same = clip == key_clip
 
-    lane = lax.broadcasted_iota(jnp.int32, (rows, width - half), 1)
+    loads[2].wait()
+    loads[3].wait()
+    lane = lax.broadcasted_iota(jnp.int32, (width - half, rows), 0)
     base = jnp.zeros(lane.shape, jnp.int32)
     for part in range(1, parts):
         base = base + jnp.where(lane >= part * n_experts, n_experts, 0)
     wanted = lane - base
     weight = jnp.zeros(lane.shape, jnp.float32)
-    for slot in range(ids_ref.shape[1]):
+    for slot in range(ids_ref.shape[0]):
         weight = weight + jnp.where(
-            ids_ref[:, slot : slot + 1] == wanted, mix_ref[:, slot : slot + 1], 0.0
+            ids_ref[slot : slot + 1, :] == wanted, mix_ref[slot : slot + 1, :], 0.0
         )
     packed = jnp.zeros(lane.shape, jnp.float32)
     for part in range(parts):
         piece = weight.astype(jnp.bfloat16).astype(jnp.float32)
         packed = jnp.where(base == part * n_experts, piece, packed)
         weight = weight - piece
-    held[q_own, c, z, :, half:width] = packed.astype(jnp.bfloat16)
-
+    unit = lax.broadcasted_iota(jnp.int32, (rows, rows), 0) == lax.broadcasted_iota(
+        jnp.int32, (rows, rows), 1
+    )
+    held[q_own, c, z, :, half:width] = lax.dot_general(
+        jnp.where(unit, 1.0, 0.0).astype(jnp.bfloat16),
+        packed.astype(jnp.bfloat16),
+        (((1,), (1,)), ((), ())),
+        preferred_element_type=jnp.float32,
+    ).astype(jnp.bfloat16)
+
+    loads[1].wait()
     for block in range(n_z):
         keys_y(block, 1 - y).wait_recv()
     keys = kv[:, :, 0:head].reshape(n_keys, head)
     values = kv[:, :, head:pair_width].reshape(n_keys, head)
-    scale = head ** (-0.5)
+    scale = head ** (-0.5) * math.log2(math.e)
     for at in range(0, queries_ref.shape[1], 2 * head):
         two = jnp.concatenate(
             [queries_ref[:, at : at + head], queries_ref[:, at + head : at + 2 * head]], axis=0
@@ -229,9 +265,9 @@
         scores = lax.dot_general(
             two, keys, (((1,), (1,)), ((), ())), preferred_element_type=jnp.float32
         )
-        scores = jnp.where(same, scores * scale, -1e30)
+        scores = jnp.where(same, scores, -1e30)
         top = jnp.max(scores, axis=1, keepdims=True)
-        weights = jnp.exp(scores - top)
+        weights = jnp.exp2((scores - top) * scale)
         total = jnp.sum(weights, axis=1, keepdims=True)
         numer = jnp.dot(
             weights.astype(jnp.bfloat16), values, preferred_element_type=jnp.float32
@@ -260,7 +296,7 @@
             x_peer,
         )
 
-    load_o.wait()
+    loads[6].wait()
     for part in range(2):
         for at in range(part * cut, (part + 1) * cut, quarter):
             result = jnp.dot(
@@ -279,6 +315,8 @@
             + sib_in[1 - x, :, columns].astype(jnp.float32)
         ).astype(jnp.bfloat16)
         proj_x(part).start()
+    loads[4].wait()
+    loads[5].wait()
     for part in range(2):
         columns = pl.ds(part * cut, cut)
         hidden_ref[:, columns] = (
@@ -305,29 +343,43 @@
             pl.when(z >= 1)(lambda: along_z(block, False).start())
         over_x(q_own, block).start()
         over_y(q_own, block).start()
+        share(q_own, c, 0, block).start()
 
     def arrive_xy(block, side):
         over_x(q_x, block).wait_recv()
         diag_y(q_x, block).start()
+        share(q_x, c, 1, block).start()
         over_y(q_y, block).wait_recv()
         diag_x(q_y, block).start()
+        share(q_y, c, 2, block).start()
+
+    def arrive_diag(block, side):
+        diag_x(q_d, block).wait_recv()
+        diag_y(q_d, block).wait_recv()
+        share(q_d, c, 3, block).start()
 
     for distance in range(n_z + 1):
         if distance < n_z:
             each_at(distance, arrive_z)
-        if distance == n_z - 1:
-            share(q_own, c, 0).start()
         if distance >= 1:
             each_at(distance - 1, arrive_xy)
-    share(q_x, c, 1).start()
-    share(q_y, c, 2).start()
-    load_gu.wait()
-    load_d.wait()
+    loads[7].wait()
+    loads[8].wait()
 
     mine = ep * lax.axis_size("tp") + tp
     many = 2 * n_z * rows
 
-    def compute(q):
+    def pair(q, slot, part):
+        columns = pl.ds(part * cut, cut)
+        return remote(
+            term.at[q, 1 - c, :, columns],
+            pair_in.at[slot, :, columns],
+            pair_send.at[slot, part],
+            pair_recv.at[slot, part],
+            sib,
+        )
+
+    def compute(q, slot):
         both = jnp.dot(
             held[q, :, :, :, 0:half].reshape(many, half),
             wgu[...],
@@ -352,19 +404,15 @@
                 .astype(jnp.bfloat16)
                 .reshape(2, n_z * rows, tile)
             )
-
-    def pair(q, slot):
-        return remote(
-            term.at[q, 1 - c], pair_in.at[slot], sib_send.at[4 + slot], sib_recv.at[4 + slot], sib
-        )
-
-    def add_pair(q, slot):
-        pair(q, slot).wait_recv()
-        for at in range(0, half, cut):
-            to = pl.ds(at, cut)
-            term[q, c, :, to] = (
-                term[q, c, :, to].astype(jnp.float32) + pair_in[slot, :, to].astype(jnp.float32)
-            ).astype(jnp.bfloat16)
+            if (at + tile) % cut == 0:
+                pair(q, slot, at // cut).start()
+
+    def add_pair(q, slot, part):
+        pair(q, slot, part).wait_recv()
+        to = pl.ds(part * cut, cut)
+        term[q, c, :, to] = (
+            term[q, c, :, to].astype(jnp.float32) + pair_in[slot, :, to].astype(jnp.float32)
+        ).astype(jnp.bfloat16)
 
     def reduce_x(q, columns, into, slot):
         return remote(term.at[q, c, :, columns], into, r_send.at[slot], r_recv.at[slot], x_peer)
@@ -381,31 +429,30 @@
     last_x = [reduce_x(q_x, high[i], from_x.at[1, :, low[i]], 6 + i) for i in range(2)]
     last_y = [reduce_y(q_y, low[i], from_y.at[0, :, low[i]], 8 + i) for i in range(2)]
 
-    share(q_own, 1 - c, 0).wait_recv()
-    compute(q_own)
-    pair(q_own, 0).start()
-    share(q_x, 1 - c, 1).wait_recv()
-    compute(q_x)
-    pair(q_x, 1).start()
-    for block in range(n_z):
-        diag_x(q_d, block).wait_recv()
-        diag_y(q_d, block).wait_recv()
-    share(q_d, c, 3).start()
-    share(q_y, 1 - c, 2).wait_recv()
-    compute(q_y)
-    pair(q_y, 2).start()
-    add_pair(q_x, 1)
+    shares_arrive(q_x, 1)
+    compute(q_x, 1)
+    shares_arrive(q_y, 2)
+    compute(q_y, 2)
+    add_pair(q_x, 1, 0)
     own_x.start()
-    share(q_d, 1 - c, 3).wait_recv()
-    compute(q_d)
-    pair(q_d, 3).start()
-    add_pair(q_y, 2)
+    add_pair(q_y, 2, 1)
     own_y.start()
-    add_pair(q_d, 3)
-    for i in range(2):
-        pass_x[i].start()
-        pass_y[i].start()
-    add_pair(q_own, 0)
+    for distance in range(n_z):
+        each_at(distance, arrive_diag)
+    shares_arrive(q_own, 0)
+    compute(q_own, 0)
+    shares_arrive(q_d, 3)
+    compute(q_d, 3)
+    add_pair(q_d, 3, 0)
+    for copy in pass_x:
+        copy.start()
+    add_pair(q_d, 3, 1)
+    for copy in pass_y:
+        copy.start()
+    add_pair(q_y, 2, 0)
+    add_pair(q_x, 1, 1)
+    add_pair(q_own, 0, 0)
+    add_pair(q_own, 0, 1)
 
     for i in range(2):
         pass_x[i].wait_recv()
@@ -470,8 +517,10 @@
         proj_pair(part).wait_send()
         proj_x(part).wait_send()
     for slot, q in enumerate((q_own, q_x, q_y, q_d)):
-        share(q, c, slot).wait_send()
-        pair(q, slot).wait_send()
+        for block in range(n_z):
+            share(q, c, slot, block).wait_send()
+        for part in range(2):
+            pair(q, slot, part).wait_send()
     for step in range(1, n_z):
         for i in range(2):
             for side in range(2):
@@ -516,10 +565,14 @@
         functools.partial(layer_kernel, n_z, n_experts, parts),
         out_shape=jax.ShapeDtypeStruct((rows, half), bf16),
         in_specs=[pl.BlockSpec(memory_space=pltpu.SMEM)]
-        + [in_vmem] * 6
-        + [pl.BlockSpec(memory_space=pl.ANY)] * 3,
+        + [pl.BlockSpec(memory_space=pltpu.HBM)] * 9,
         out_specs=in_vmem,
         scratch_shapes=[
+            pltpu.VMEM(queries.shape, bf16),
+            pltpu.VMEM(residual.shape, bf16),
+            pltpu.VMEM((1, half), jnp.float32),
+            pltpu.VMEM(expert_ids.shape[::-1], jnp.int32),
+            pltpu.VMEM(mix_weights.shape[::-1], jnp.float32),
             pltpu.VMEM((n_ep, q_rows, 2 * HD), bf16),
             pltpu.VMEM(queries.shape, bf16),
             pltpu.VMEM((2, 2, rows, half), bf16),
@@ -543,15 +596,16 @@
             pltpu.VMEM((2, many, cut), bf16),
             pltpu.VMEM((2, many, cut), bf16),
             pltpu.VMEM((2, 2, n_z - 1, rows, cut // 2), bf16),
-            dma((3,)),
+            dma((9,)),
             dma((2, n_z)),
         ]
         + [dma((n_z,))] * 9
-        + [dma((8,))] * 2
+        + [dma((4, n_z))] * 2
+        + [dma((4, 2))] * 2
         + [dma((10,))] * 2
         + [dma((2, 2, n_z - 1))] * 2,
         compiler_params=pltpu.CompilerParams(
-            collective_id=0, has_side_effects=True, vmem_limit_bytes=48 * 1024 * 1024
+            collective_id=0, has_side_effects=True, vmem_limit_bytes=62 * 1024 * 1024
         ),
     )(
         clip_lengths,
@@ -559,8 +613,8 @@
         keys_values,
         residual,
         norm_gain.reshape(1, half),
-        expert_ids,
-        mix_weights,
+        expert_ids.T,
+        mix_weights.T,
         w_out,
         w_gate_up,
         w_down,

time: 94.1 us -> 83.3 us (0.89)
  local copies, waits for them, and re-layouts: 9.63 us -> 1.57 us
  Pallas kernels: 84.1 us -> 81.6 us
    unnamed x17 -> x1, local copies, waits for them, and re-layouts: 9.63 us -> 1.57 us
    pallas_call x1, Pallas kernels: 84.1 us -> 81.6 us  [whole_layer(): pl.pallas_call(functools.partial(layer_kernel, n_z, n_experts, parts), ou...]
where the time goes in v3:
time: 83.3 us; the launch traced here: 83.2 us
  Pallas kernels  81.6 us (98%)
  local copies, waits for them, and re-layouts  1.57 us (2%)
    pallas_call x1, Pallas kernels, whole_layer(): pl.pallas_call(functools.partial(layer_kernel, n_z, n_experts, parts), ou...  81.6 us

profile of v3, /device:TPU:0, one launch (start us, length us, event | category | flops | bytes accessed | tf_op | source)
XLA Modules:
  0.0 83.2 jit_solution(2640372403141440542)
XLA Ops:
  0.0 81.6 %shard_map.100 = bf16[32,2048]{1,0:T(8,128)(2,1)} custom-call(s32[3]{0:T(128)} %clip_ref.1, bf16[128,1024]{1,0:T(8,128)(2,1)} %queries_hbm.1, bf16[128,1024]{1,0:T(8,128)(2,1)} %kv_hbm.1, bf16[32,2048]{1,0:T(8,128)(2,1)} %residual_hbm.1, f32[1,2048]{1,0:T(1,128)} %bitcast.3, s32[8,32]{1,0:T(8,128)} %bitcast.4, f32[8,32]{1,0:T(8,128)} %bitcast.5, ...), custom_call_target="tpu_custom_call" | custom-call | tf_op jit(solution)/shard_map/pallas_call | solution.py:564
  81.6 1.6 %copy.12 = bf16[32,2048]{1,0:T(8,128)(2,1)} copy(bf16[32,2048]{1,0:T(8,128)(2,1)} %shard_map.100) | data formatting | bytes 262144

commit v4 on v3

--- a/solution.py
+++ b/solution.py
@@ -23,7 +23,7 @@
     n_z,
     n_experts,
     parts,
-    clip_ref,
+    clip_hbm,
     queries_hbm,
     kv_hbm,
     residual_hbm,
@@ -34,6 +34,7 @@
     wgu_hbm,
     wd_hbm,
     out_ref,
+    clip_ref,
     queries_ref,
     residual_ref,
     gain_ref,
@@ -113,6 +114,7 @@
                 (wo_hbm, wo),
                 (wgu_hbm.at[0], wgu),
                 (wd_hbm.at[0], wd),
+                (clip_hbm, clip_ref),
             )
         )
     ]
@@ -219,6 +221,7 @@
     clip = jnp.zeros(place.shape, jnp.int32)
     key_clip = jnp.zeros(key_place.shape, jnp.int32)
     end = jnp.int32(0)
+    loads[9].wait()
     for number in range(clip_ref.shape[0]):
         end = end + clip_ref[number]
         clip = clip + jnp.where(place >= end, 1, 0)
@@ -358,14 +361,6 @@
         diag_y(q_d, block).wait_recv()
         share(q_d, c, 3, block).start()
 
-    for distance in range(n_z + 1):
-        if distance < n_z:
-            each_at(distance, arrive_z)
-        if distance >= 1:
-            each_at(distance - 1, arrive_xy)
-    loads[7].wait()
-    loads[8].wait()
-
     mine = ep * lax.axis_size("tp") + tp
     many = 2 * n_z * rows
 
@@ -420,41 +415,52 @@
     def reduce_y(q, columns, into, slot):
         return remote(term.at[q, c, :, columns], into, r_send.at[slot], r_recv.at[slot], y_peer)
 
-    low = [pl.ds(0, quarter), pl.ds(quarter, quarter)]
-    high = [pl.ds(cut, quarter), pl.ds(cut + quarter, quarter)]
+    chunks = from_z.shape[1]
+    piece_width = cut // chunks
+    low = [pl.ds(i * piece_width, piece_width) for i in range(chunks)]
+    high = [pl.ds(cut + i * piece_width, piece_width) for i in range(chunks)]
     own_x = reduce_x(q_x, first, from_x.at[0], 0)
     own_y = reduce_y(q_y, second, from_y.at[1], 1)
-    pass_x = [reduce_x(q_d, low[i], relay_x.at[:, low[i]], 2 + i) for i in range(2)]
-    pass_y = [reduce_y(q_d, high[i], relay_y.at[:, low[i]], 4 + i) for i in range(2)]
-    last_x = [reduce_x(q_x, high[i], from_x.at[1, :, low[i]], 6 + i) for i in range(2)]
-    last_y = [reduce_y(q_y, low[i], from_y.at[0, :, low[i]], 8 + i) for i in range(2)]
-
+    pass_x = [reduce_x(q_d, low[i], relay_x.at[:, low[i]], 2 + i) for i in range(chunks)]
+    pass_y = [reduce_y(q_d, high[i], relay_y.at[:, low[i]], 6 + i) for i in range(chunks)]
+    last_x = [reduce_x(q_x, high[i], from_x.at[1, :, low[i]], 10 + i) for i in range(chunks)]
+    last_y = [reduce_y(q_y, low[i], from_y.at[0, :, low[i]], 14 + i) for i in range(chunks)]
+
+    for distance in range(n_z):
+        each_at(distance, arrive_z)
+        if distance >= 1:
+            each_at(distance - 1, arrive_xy)
+    loads[7].wait()
+    loads[8].wait()
+    shares_arrive(q_own, 0)
+    compute(q_own, 0)
+    each_at(n_z - 1, arrive_xy)
     shares_arrive(q_x, 1)
     compute(q_x, 1)
+    for distance in range(n_z - 2):
+        each_at(distance, arrive_diag)
     shares_arrive(q_y, 2)
-    compute(q_y, 2)
     add_pair(q_x, 1, 0)
     own_x.start()
+    compute(q_y, 2)
+    for distance in range(max(n_z - 2, 0), n_z):
+        each_at(distance, arrive_diag)
     add_pair(q_y, 2, 1)
     own_y.start()
-    for distance in range(n_z):
-        each_at(distance, arrive_diag)
-    shares_arrive(q_own, 0)
-    compute(q_own, 0)
     shares_arrive(q_d, 3)
     compute(q_d, 3)
     add_pair(q_d, 3, 0)
-    for copy in pass_x:
+    for copy in pass_x[:2]:
         copy.start()
     add_pair(q_d, 3, 1)
-    for copy in pass_y:
+    for copy in pass_y[:2]:
         copy.start()
     add_pair(q_y, 2, 0)
     add_pair(q_x, 1, 1)
     add_pair(q_own, 0, 0)
     add_pair(q_own, 0, 1)
 
-    for i in range(2):
+    def relay(i):
         pass_x[i].wait_recv()
         term[q_y, c, :, low[i]] = (
             term[q_y, c, :, low[i]].astype(jnp.float32) + relay_x[:, low[i]].astype(jnp.float32)
@@ -465,6 +471,9 @@
             term[q_x, c, :, high[i]].astype(jnp.float32) + relay_y[:, low[i]].astype(jnp.float32)
         ).astype(jnp.bfloat16)
         last_x[i].start()
+        if i + 2 < chunks:
+            pass_x[i + 2].start()
+            pass_y[i + 2].start()
 
     def finish(side, i):
         columns = high[i] if side else low[i]
@@ -499,15 +508,21 @@
             total = total + from_z[side, i, n_z - 1 - step].astype(jnp.float32)
         out_ref[:, columns] = total.astype(jnp.bfloat16)
 
-    own_x.wait_recv()
-    own_y.wait_recv()
-    for i in range(2):
+    def complete(i):
         for side in range(2):
             (last_x if side else last_y)[i].wait_recv()
             finish(side, i)
             for step in range(1, n_z):
                 deliver(side, i, step).start()
-    for i in range(2):
+
+    relay(0)
+    own_x.wait_recv()
+    own_y.wait_recv()
+    for i in range(1, chunks):
+        relay(i)
+        complete(i - 1)
+    complete(chunks - 1)
+    for i in range(chunks):
         for side in range(2):
             collect(side, i)
 
@@ -522,7 +537,7 @@
         for part in range(2):
             pair(q, slot, part).wait_send()
     for step in range(1, n_z):
-        for i in range(2):
+        for i in range(chunks):
             for side in range(2):
                 deliver(side, i, step).wait_send()
     for block in range(n_z):
@@ -558,16 +573,17 @@
     width = half + -(-parts * n_experts // 128) * 128
     many = n_z * rows
     cut = half // 2
+    chunks = 4
     dma = pltpu.SemaphoreType.DMA
     bf16 = jnp.bfloat16
     in_vmem = pl.BlockSpec(memory_space=pltpu.VMEM)
     return pl.pallas_call(
         functools.partial(layer_kernel, n_z, n_experts, parts),
         out_shape=jax.ShapeDtypeStruct((rows, half), bf16),
-        in_specs=[pl.BlockSpec(memory_space=pltpu.SMEM)]
-        + [pl.BlockSpec(memory_space=pltpu.HBM)] * 9,
+        in_specs=[pl.BlockSpec(memory_space=pltpu.HBM)] * 10,
         out_specs=in_vmem,
         scratch_shapes=[
+            pltpu.SMEM(clip_lengths.shape, jnp.int32),
             pltpu.VMEM(queries.shape, bf16),
             pltpu.VMEM(residual.shape, bf16),
             pltpu.VMEM((1, half), jnp.float32),
@@ -595,15 +611,15 @@
             pltpu.VMEM((many, cut), bf16),
             pltpu.VMEM((2, many, cut), bf16),
             pltpu.VMEM((2, many, cut), bf16),
-            pltpu.VMEM((2, 2, n_z - 1, rows, cut // 2), bf16),
-            dma((9,)),
+            pltpu.VMEM((2, chunks, n_z - 1, rows, cut // chunks), bf16),
+            dma((10,)),
             dma((2, n_z)),
         ]
         + [dma((n_z,))] * 9
         + [dma((4, n_z))] * 2
         + [dma((4, 2))] * 2
-        + [dma((10,))] * 2
-        + [dma((2, 2, n_z - 1))] * 2,
+        + [dma((2 + 4 * chunks,))] * 2
+        + [dma((2, chunks, n_z - 1))] * 2,
         compiler_params=pltpu.CompilerParams(
             collective_id=0, has_side_effects=True, vmem_limit_bytes=62 * 1024 * 1024
         ),

time: 83.3 us -> 81.8 us (0.982)
  Pallas kernels: 81.6 us -> 80.1 us
    pallas_call x1, Pallas kernels: 81.6 us -> 80.1 us  [whole_layer(): pl.pallas_call(functools.partial(layer_kernel, n_z, n_experts, parts), ou...]
where the time goes in v4:
time: 81.8 us; the launch traced here: 81.7 us
  Pallas kernels  80.1 us (98%)
  local copies, waits for them, and re-layouts  1.57 us (2%)
    pallas_call x1, Pallas kernels, whole_layer(): pl.pallas_call(functools.partial(layer_kernel, n_z, n_experts, parts), ou...  80.1 us

profile of v4, /device:TPU:0, one launch (start us, length us, event | category | flops | bytes accessed | tf_op | source)
XLA Modules:
  0.0 81.7 jit_solution(3483186926277005119)
XLA Ops:
  0.0 80.1 %shard_map.100 = bf16[32,2048]{1,0:T(8,128)(2,1)} custom-call(s32[3]{0:T(128)} %clip_hbm.1, bf16[128,1024]{1,0:T(8,128)(2,1)} %queries_hbm.1, bf16[128,1024]{1,0:T(8,128)(2,1)} %kv_hbm.1, bf16[32,2048]{1,0:T(8,128)(2,1)} %residual_hbm.1, f32[1,2048]{1,0:T(1,128)} %bitcast.3, s32[8,32]{1,0:T(8,128)} %bitcast.4, f32[8,32]{1,0:T(8,128)} %bitcast.5, ...), custom_call_target="tpu_custom_call" | custom-call | tf_op jit(solution)/shard_map/pallas_call | solution.py:580
  80.1 1.6 %copy.12 = bf16[32,2048]{1,0:T(8,128)(2,1)} copy(bf16[32,2048]{1,0:T(8,128)(2,1)} %shard_map.100) | data formatting | bytes 262144

commit v5 on v4

--- a/solution.py
+++ b/solution.py
@@ -42,6 +42,9 @@
     mix_ref,
     kv,
     attended,
+    tops,
+    totals,
+    numers,
     proj,
     sib_in,
     x_in,
@@ -211,22 +214,25 @@
     head = pair_width // 2
     loads[0].wait()
     pl.semaphore_wait(barrier, 3 + n_z - 1)
-    for distance in range(n_z):
+    for distance in range(min(2, n_z)):
         each_at(distance, keys_arrive)
 
-    n_keys = 2 * n_z * q_rows
+    near = z // (n_z // 2)
+    n_keys = n_z * q_rows
     place = lax.broadcasted_iota(jnp.int32, (2 * q_rows, 1), 0)
     place = jnp.where(place >= q_rows, place - q_rows, place) + ep * q_rows
     key_place = lax.broadcasted_iota(jnp.int32, (1, n_keys), 1)
     clip = jnp.zeros(place.shape, jnp.int32)
-    key_clip = jnp.zeros(key_place.shape, jnp.int32)
+    key_clips = [jnp.zeros(key_place.shape, jnp.int32) for _ in range(2)]
+    key_places = [key_place + near * n_keys, key_place + (1 - near) * n_keys]
     end = jnp.int32(0)
     loads[9].wait()
     for number in range(clip_ref.shape[0]):
         end = end + clip_ref[number]
         clip = clip + jnp.where(place >= end, 1, 0)
-        key_clip = key_clip + jnp.where(key_place >= end, 1, 0)
-    same = clip == key_clip
+        key_clips = [
+            key_clip + jnp.where(at >= end, 1, 0) for key_clip, at in zip(key_clips, key_places)
+        ]
 
     loads[2].wait()
     loads[3].wait()
@@ -256,28 +262,57 @@
     ).astype(jnp.bfloat16)
 
     loads[1].wait()
-    for block in range(n_z):
-        keys_y(block, 1 - y).wait_recv()
-    keys = kv[:, :, 0:head].reshape(n_keys, head)
-    values = kv[:, :, head:pair_width].reshape(n_keys, head)
     scale = head ** (-0.5) * math.log2(math.e)
-    for at in range(0, queries_ref.shape[1], 2 * head):
-        two = jnp.concatenate(
-            [queries_ref[:, at : at + head], queries_ref[:, at + head : at + 2 * head]], axis=0
-        )
-        scores = lax.dot_general(
-            two, keys, (((1,), (1,)), ((), ())), preferred_element_type=jnp.float32
-        )
-        scores = jnp.where(same, scores, -1e30)
-        top = jnp.max(scores, axis=1, keepdims=True)
-        weights = jnp.exp2((scores - top) * scale)
-        total = jnp.sum(weights, axis=1, keepdims=True)
-        numer = jnp.dot(
-            weights.astype(jnp.bfloat16), values, preferred_element_type=jnp.float32
-        )
-        result = (numer / total).astype(jnp.bfloat16)
-        attended[:, at : at + head] = result[0:q_rows]
-        attended[:, at + head : at + 2 * head] = result[q_rows : 2 * q_rows]
+
+    def attend(far):
+        side = (1 - near) if far else near
+        first_block = pl.ds(side * n_z, n_z)
+        keys = kv[first_block, :, 0:head].reshape(n_keys, head)
+        values = kv[first_block, :, head:pair_width].reshape(n_keys, head)
+        same = clip == key_clips[1 if far else 0]
+        for at in range(0, queries_ref.shape[1], 2 * head):
+            slot = at // (2 * head)
+            two = jnp.concatenate(
+                [queries_ref[:, at : at + head], queries_ref[:, at + head : at + 2 * head]],
+                axis=0,
+            )
+            scores = lax.dot_general(
+                two, keys, (((1,), (1,)), ((), ())), preferred_element_type=jnp.float32
+            )
+            scores = jnp.where(same, scores, -1e30)
+            top = jnp.max(scores, axis=1, keepdims=True)
+            if far:
+                top = jnp.maximum(top, tops[slot])
+            weights = jnp.exp2((scores - top) * scale)
+            total = jnp.sum(weights, axis=1, keepdims=True)
+            numer = jnp.dot(
+                weights.astype(jnp.bfloat16), values, preferred_element_type=jnp.float32
+            )
+            if not far:
+                tops[slot] = top
+                totals[slot] = total
+                numers[slot] = numer
+                if slot % 2 == 1 and later:
+                    each_at(later.pop(0), keys_arrive)
+                continue
+            factor = jnp.exp2((tops[slot] - top) * scale)
+            total = total + totals[slot] * factor
+            result = ((numer + numers[slot] * factor) / total).astype(jnp.bfloat16)
+            attended[:, at : at + head] = result[0:q_rows]
+            attended[:, at + head : at + 2 * head] = result[q_rows : 2 * q_rows]
+
+    half_z = n_z // 2
+    for distance in range(2, half_z):
+        each_at(distance, keys_arrive)
+    for block in range(half_z):
+        keys_y(near * half_z + block, 1 - y).wait_recv()
+    later = list(range(max(2, half_z), n_z))
+    attend(False)
+    for distance in later:
+        each_at(distance, keys_arrive)
+    for block in range(half_z):
+        keys_y((1 - near) * half_z + block, 1 - y).wait_recv()
+    attend(True)
 
     def proj_pair(part):
         columns = pl.ds(part * cut, cut)
@@ -591,6 +626,9 @@
             pltpu.VMEM(mix_weights.shape[::-1], jnp.float32),
             pltpu.VMEM((n_ep, q_rows, 2 * HD), bf16),
             pltpu.VMEM(queries.shape, bf16),
+            pltpu.VMEM((queries.shape[1] // (2 * HD), 2 * q_rows, 1), jnp.float32),
+            pltpu.VMEM((queries.shape[1] // (2 * HD), 2 * q_rows, 1), jnp.float32),
+            pltpu.VMEM((queries.shape[1] // (2 * HD), 2 * q_rows, HD), jnp.float32),
             pltpu.VMEM((2, 2, rows, half), bf16),
             pltpu.VMEM((2, rows, half), bf16),
             pltpu.VMEM((rows, half), bf16),
@@ -654,8 +692,7 @@
     if (
         lax.axis_size("pool") == 1
         and lax.axis_size("tp") == 4
-        and lax.axis_size("ep") % 2 == 0
-        and lax.axis_size("ep") > 2
+        and lax.axis_size("ep") % 4 == 0
         and heads_here == QH // KVH
         and w_gate_up.shape[0] == 1
         and residual.shape[0] % 16 == 0

time: 81.8 us -> 82.5 us (level)
  no operation moved by 1% of the time
where the time goes in v5:
time: 82.5 us; the launch traced here: 82.3 us
  Pallas kernels  80.7 us (98%)
  local copies, waits for them, and re-layouts  1.57 us (2%)
    pallas_call x1, Pallas kernels, whole_layer(): pl.pallas_call(functools.partial(layer_kernel, n_z, n_experts, parts), ou...  80.7 us

profile of v5, /device:TPU:0, one launch (start us, length us, event | category | flops | bytes accessed | tf_op | source)
XLA Modules:
  0.0 82.3 jit_solution(14583442854794868631)
XLA Ops:
  0.0 80.7 %shard_map.100 = bf16[32,2048]{1,0:T(8,128)(2,1)} custom-call(s32[3]{0:T(128)} %clip_hbm.1, bf16[128,1024]{1,0:T(8,128)(2,1)} %queries_hbm.1, bf16[128,1024]{1,0:T(8,128)(2,1)} %kv_hbm.1, bf16[32,2048]{1,0:T(8,128)(2,1)} %residual_hbm.1, f32[1,2048]{1,0:T(1,128)} %bitcast.3, s32[8,32]{1,0:T(8,128)} %bitcast.4, f32[8,32]{1,0:T(8,128)} %bitcast.5, ...), custom_call_target="tpu_custom_call" | custom-call | tf_op jit(solution)/shard_map/pallas_call | solution.py:615
  80.7 1.6 %copy.12 = bf16[32,2048]{1,0:T(8,128)(2,1)} copy(bf16[32,2048]{1,0:T(8,128)(2,1)} %shard_map.100) | data formatting | bytes 262144

commit v6 on v4

--- a/solution.py
+++ b/solution.py
@@ -188,12 +188,15 @@
         pl.when(z - distance >= 0)(lambda: act(z - distance, -1))
         pl.when(z + distance < n_z)(lambda: act(z + distance, 1))
 
-    def keys_z(block, up):
-        there = z + 1 if up else z - 1
+    def keys_z(step):
+        there = (z + step) % n_z
+        return remote(
+            kv.at[ep], kv.at[ep], kz_send.at[step], kz_recv.at[z], (there * 2 + y, tp)
+        )
+
+    def keys_from(block):
         here = kv.at[block * 2 + y]
-        return remote(
-            here, here, kz_send.at[1 if up else 0, block], kz_recv.at[block], (there * 2 + y, tp)
-        )
+        return remote(here, here, kz_send.at[0], kz_recv.at[block], y_peer)
 
     def keys_y(block, side_y):
         here = kv.at[block * 2 + side_y]
@@ -201,16 +204,14 @@
 
     def keys_arrive(block, side):
         if side:
-            keys_z(block, side < 0).wait_recv()
-        if side <= 0:
-            pl.when(z + 1 < n_z)(lambda: keys_z(block, True).start())
-        if side >= 0:
-            pl.when(z >= 1)(lambda: keys_z(block, False).start())
+            keys_from(block).wait_recv()
         keys_y(block, y).start()
 
     head = pair_width // 2
     loads[0].wait()
     pl.semaphore_wait(barrier, 3 + n_z - 1)
+    for step in sorted(range(1, n_z), key=lambda step: min(step, n_z - step)):
+        keys_z(step).start()
     for distance in range(n_z):
         each_at(distance, keys_arrive)
 
@@ -280,7 +281,7 @@
         attended[:, at + head : at + 2 * head] = result[q_rows : 2 * q_rows]
 
     def proj_pair(part):
-        columns = pl.ds(part * cut, cut)
+        columns = pl.ds(part * quarter, quarter)
         return remote(
             proj.at[1 - c, :, :, columns],
             sib_in.at[:, :, columns],
@@ -290,18 +291,18 @@
         )
 
     def proj_x(part):
-        columns = pl.ds(part * cut, cut)
+        columns = pl.ds(part * quarter, quarter)
         return remote(
             proj.at[c, 1 - x, :, columns],
             x_in.at[:, columns],
-            at_send.at[2 + part],
-            at_recv.at[2 + part],
+            at_send.at[4 + part],
+            at_recv.at[4 + part],
             x_peer,
         )
 
     loads[6].wait()
-    for part in range(2):
-        for at in range(part * cut, (part + 1) * cut, quarter):
+    for part in range(4):
+        for at in [part * quarter]:
             result = jnp.dot(
                 attended[...], wo[:, at : at + quarter], preferred_element_type=jnp.float32
             ).astype(jnp.bfloat16)
@@ -310,8 +311,8 @@
                     start = (side_x * 2 + side_c) * rows
                     proj[side_c, side_x, :, at : at + quarter] = result[start : start + rows]
         proj_pair(part).start()
-    for part in range(2):
-        columns = pl.ds(part * cut, cut)
+    for part in range(4):
+        columns = pl.ds(part * quarter, quarter)
         proj_pair(part).wait_recv()
         proj[c, 1 - x, :, columns] = (
             proj[c, 1 - x, :, columns].astype(jnp.float32)
@@ -320,15 +321,15 @@
         proj_x(part).start()
     loads[4].wait()
     loads[5].wait()
-    for part in range(2):
-        columns = pl.ds(part * cut, cut)
+    for part in range(4):
+        columns = pl.ds(part * quarter, quarter)
         hidden_ref[:, columns] = (
             residual_ref[:, columns].astype(jnp.float32)
             + proj[c, x, :, columns].astype(jnp.float32)
             + sib_in[x, :, columns].astype(jnp.float32)
         )
-    for part in range(2):
-        columns = pl.ds(part * cut, cut)
+    for part in range(4):
+        columns = pl.ds(part * quarter, quarter)
         proj_x(part).wait_recv()
         hidden_ref[:, columns] += x_in[:, columns].astype(jnp.float32)
     hidden = hidden_ref[...]
@@ -528,7 +529,9 @@
 
     for copy in [own_x, own_y] + pass_x + pass_y + last_x + last_y:
         copy.wait_send()
-    for part in range(2):
+    for step in range(1, n_z):
+        keys_z(step).wait_send()
+    for part in range(4):
         proj_pair(part).wait_send()
         proj_x(part).wait_send()
     for slot, q in enumerate((q_own, q_x, q_y, q_d)):
@@ -542,8 +545,6 @@
                 deliver(side, i, step).wait_send()
     for block in range(n_z):
         keys_y(block, y).wait_send()
-        pl.when((z + 1 < n_z) & (block <= z))(lambda: keys_z(block, True).wait_send())
-        pl.when((z >= 1) & (block >= z))(lambda: keys_z(block, False).wait_send())
         over_x(q_own, block).wait_send()
         over_y(q_own, block).wait_send()
         diag_x(q_y, block).wait_send()
@@ -596,12 +597,12 @@
             pltpu.VMEM((rows, half), bf16),
             pltpu.VMEM((rows, half), jnp.float32),
             pltpu.VMEM(w_out.shape, bf16),
-            dma((2, n_z)),
             dma((n_z,)),
             dma((n_z,)),
             dma((n_z,)),
-            dma((4,)),
-            dma((4,)),
+            dma((n_z,)),
+            dma((8,)),
+            dma((8,)),
             pltpu.VMEM((4, 2, n_z, rows, width), bf16),
             pltpu.VMEM(w_gate_up.shape[1:], bf16),
             pltpu.VMEM(w_down.shape[1:], bf16),

time: 81.8 us -> 79.9 us (0.977)
  Pallas kernels: 80.1 us -> 78.2 us
    pallas_call x1, Pallas kernels: 80.1 us -> 78.2 us  [whole_layer(): pl.pallas_call(functools.partial(layer_kernel, n_z, n_experts, parts), ou...]
where the time goes in v6:
time: 79.9 us; the launch traced here: 79.8 us
  Pallas kernels  78.2 us (98%)
  local copies, waits for them, and re-layouts  1.57 us (2%)
    pallas_call x1, Pallas kernels, whole_layer(): pl.pallas_call(functools.partial(layer_kernel, n_z, n_experts, parts), ou...  78.2 us

profile of v6, /device:TPU:0, one launch (start us, length us, event | category | flops | bytes accessed | tf_op | source)
XLA Modules:
  0.0 79.8 jit_solution(306366025813542677)
XLA Ops:
  0.0 78.2 %shard_map.100 = bf16[32,2048]{1,0:T(8,128)(2,1)} custom-call(s32[3]{0:T(128)} %clip_hbm.1, bf16[128,1024]{1,0:T(8,128)(2,1)} %queries_hbm.1, bf16[128,1024]{1,0:T(8,128)(2,1)} %kv_hbm.1, bf16[32,2048]{1,0:T(8,128)(2,1)} %residual_hbm.1, f32[1,2048]{1,0:T(1,128)} %bitcast.3, s32[8,32]{1,0:T(8,128)} %bitcast.4, f32[8,32]{1,0:T(8,128)} %bitcast.5, ...), custom_call_target="tpu_custom_call" | custom-call | tf_op jit(solution)/shard_map/pallas_call | solution.py:581
  78.2 1.6 %copy.12 = bf16[32,2048]{1,0:T(8,128)(2,1)} copy(bf16[32,2048]{1,0:T(8,128)(2,1)} %shard_map.100) | data formatting | bytes 262144
